TPU v7x, 256 devices: a whole 4x4x8 slice. The times are simulated.
256 devices in a mesh: gx: 8 (over x, core), gy: 4 (over z_hi), gz: 8 (over y, z_lo).
Axes of the slice: x: 4, y: 4, z: 8 (z_hi: 4, z_lo: 2; z = z_hi * 2 + z_lo), core: 2. Of those that a mesh axis runs over, the one named last changes fastest.
Arguments:
- positions: float32 [3, 16384], P(None, ('gx', 'gy', 'gz')), as said below
- atom_features: float32 [16384, 256], P(('gx', 'gy', 'gz')), may hold values from -6 to 6
- species: int32 [16384], P(('gx', 'gy', 'gz')), may hold values from 0 to 3
- edge_neighbor: int32 [16384, 128], P(('gx', 'gy', 'gz')), may hold values from 0 to 1338, as said below
- edge_live: int32 [16384, 128], P(('gx', 'gy', 'gz')), may hold values from 0 to 1, as said below
- send_list: int32 [6912, 48], P(('gx', 'gy', 'gz')), may hold values from 0 to 63, as said below
- species_scale: float32 [4], replicated, may hold values from 0.5 to 2
- species_shift: float32 [4], replicated, may hold values from -4 to 4
- w_center: bfloat16 [256, 256], replicated, may hold values from -0.375 to 0.375
- w_neighbor: bfloat16 [256, 256], replicated, may hold values from -0.375 to 0.375
- w_basis: bfloat16 [8, 256], replicated, may hold values from -2 to 2
- w_env: bfloat16 [256, 192], replicated, may hold values from -0.375 to 0.375
- w_latent: bfloat16 [448, 256], replicated, may hold values from -0.25 to 0.25
- w_out: bfloat16 [256, 128], replicated, may hold values from -0.375 to 0.375
- w_final: float32 [128], replicated, may hold values from -0.125 to 0.125
Outputs:
- atom_energy: float32 [16384], P(('gx', 'gy', 'gz'))
- forces: float32 [3, 16384], P(None, ('gx', 'gy', 'gz'))
- feature_grad: float32 [16384, 256], P(('gx', 'gy', 'gz'))
Inputs may be any that keep to these rules, and one draw needn't show every extreme that they name: `edge_neighbor`: row a names the 128 neighbour slots of atom a, whose device is a // 64: an index into that device's local list (owned atoms, then ghost cell c entry g at 64 + c * 48 + g); never the atom itself, never ghost cell 13, and a ghost entry only if the sender listed a real atom there. Pairs are at most three lattice sites apart along each axis. `edge_live`: slots with 0 still name another atom. `send_list`: row 27 e + c lists local indices of owned atoms of device e sent in travel direction c; a direction's list holds the atoms of the box of lattice sites that it covers (3 layers along each axis where the direction moves, the whole cell along the others), and entries past that box's size, and all of cell 13, are arbitrary owned atoms. `positions`: each device's atoms lie inside its own cell, and any two atoms, ghost images included, are at least 1.7 apart.
All inputs are finite; a program needn't handle non-finite values.
Results may differ from a plain program's by a relative error of at most 0.011.
Values may be sent and summed in bfloat16 or wider, within the bound.
A program may use at most 64 MiB of HBM per device.

v0:
```python
import math

import jax
import jax.numpy as jnp
from jax import lax
from jax.sharding import PartitionSpec as P

SIDE = 4
BLK = 4


cut_radius = 6.0
lattice_spacing = 2.15
env_norm = 0.125


def from_behind(array, axis, by):
    size = lax.axis_size(axis)
    return lax.ppermute(array, axis, [(i, (i + by) % size) for i in range(size)])


def for_sending(array):

    def short(part):
        return part.astype(jnp.bfloat16) if part.dtype == jnp.float32 else part

    return jax.tree.map(short, array)


def harmonics(unit_x, unit_y, unit_z):
    sqrt_three = math.sqrt(3.0)
    sqrt_five = math.sqrt(5.0)
    sqrt_fifteen = math.sqrt(15.0)
    degree_one = jnp.stack([sqrt_three * unit_x, sqrt_three * unit_y, sqrt_three * unit_z])
    degree_two = jnp.stack(
        [
            sqrt_fifteen * unit_x * unit_y,
            sqrt_fifteen * unit_y * unit_z,
            0.5 * sqrt_five * (3.0 * unit_z * unit_z - 1.0),
            sqrt_fifteen * unit_x * unit_z,
            0.5 * sqrt_fifteen * (unit_x * unit_x - unit_y * unit_y),
        ]
    )
    return (degree_one, degree_two)


def edge_sums(
    all_coords,
    neighbor_proj,
    center_proj,
    first_row,
    neighbor,
    live_mask,
    w_basis,
    w_env,
    w_latent,
    w_out,
    w_final,
):
    block_size, slot_count = neighbor.shape
    latent_width = center_proj.shape[1]
    channels = w_env.shape[1] // 3
    basis_count = w_basis.shape[0]
    center_coords = lax.dynamic_slice_in_dim(all_coords, first_row, block_size, 1)
    flat_index = neighbor.reshape(-1)
    other_coords = jnp.take(all_coords, flat_index, axis=1).reshape(3, block_size, slot_count)
    relative = other_coords - center_coords[:, :, None]
    distance = jnp.sqrt(jnp.sum(relative * relative, axis=0))
    unit_vec = relative / distance[None]
    scaled = distance / cut_radius
    polynomial = 1.0 - 28.0 * scaled**6 + 48.0 * scaled**7 - 21.0 * scaled**8
    envelope = jnp.where(scaled < 1.0, polynomial, 0.0) * live_mask.astype(jnp.float32)
    frequency = jnp.arange(1, basis_count + 1).astype(jnp.float32) * (math.pi / cut_radius)
    bessel = (
        math.sqrt(2.0 / cut_radius)
        * jnp.sin(distance[:, :, None] * frequency)
        / distance[:, :, None]
    )
    radial = jnp.dot(
        bessel.reshape(-1, basis_count).astype(jnp.bfloat16),
        w_basis,
        preferred_element_type=jnp.float32,
    )
    preact = (
        jnp.take(neighbor_proj, flat_index, axis=0)
        + radial
        + jnp.repeat(center_proj, slot_count, axis=0)
    )
    env_flat = envelope.reshape(-1, 1)
    latent = env_flat * jax.nn.silu(preact)
    latent_half = latent.astype(jnp.bfloat16)
    weights = jnp.dot(latent_half, w_env, preferred_element_type=jnp.float32).reshape(
        block_size, slot_count, 3, channels
    )
    degree_one, degree_two = harmonics(unit_vec[0], unit_vec[1], unit_vec[2])
    weight_zero = weights[:, :, 0]
    weight_one = weights[:, :, 1]
    weight_two = weights[:, :, 2]
    env_zero = env_norm * jnp.sum(weight_zero, axis=1)
    env_one = env_norm * jnp.sum(degree_one[:, :, :, None] * weight_one[None], axis=2)
    env_two = env_norm * jnp.sum(degree_two[:, :, :, None] * weight_two[None], axis=2)
    scalar_zero = weight_zero * env_zero[:, None, :]
    scalar_one = weight_one * jnp.sum(degree_one[:, :, :, None] * env_one[:, :, None, :], axis=0)
    scalar_two = weight_two * jnp.sum(degree_two[:, :, :, None] * env_two[:, :, None, :], axis=0)
    scalars = jnp.concatenate([scalar_zero, scalar_one, scalar_two], axis=2).reshape(
        block_size * slot_count, 3 * channels
    )
    update = jax.nn.silu(
        jnp.dot(latent_half, w_latent[:latent_width], preferred_element_type=jnp.float32)
        + jnp.dot(
            scalars.astype(jnp.bfloat16),
            w_latent[latent_width:],
            preferred_element_type=jnp.float32,
        )
    )
    refined = latent + env_flat * update
    hidden = jax.nn.silu(
        jnp.dot(refined.astype(jnp.bfloat16), w_out, preferred_element_type=jnp.float32)
    )
    edge_energy = envelope * jnp.sum(hidden * w_final, axis=1).reshape(block_size, slot_count)
    return jnp.sum(edge_energy, axis=1)


def local_terms(
    own_coords,
    own_features,
    ghost_coords,
    ghost_features,
    species,
    neighbor,
    live_mask,
    species_scale,
    species_shift,
    w_center,
    w_neighbor,
    w_basis,
    w_env,
    w_latent,
    w_out,
    w_final,
    block_size,
):
    atom_count = own_coords.shape[1]
    all_coords = jnp.concatenate([own_coords, ghost_coords], axis=1)
    all_features = jnp.concatenate([own_features, ghost_features.astype(jnp.float32)], axis=0)

    def project(features_all):
        rounded = features_all.astype(jnp.bfloat16)
        return (
            jnp.dot(rounded[:atom_count], w_center, preferred_element_type=jnp.float32),
            jnp.dot(rounded, w_neighbor, preferred_element_type=jnp.float32),
        )

    (center_proj, neighbor_proj), project_back = jax.vjp(project, all_features)
    kinds = jnp.arange(species_scale.shape[0], dtype=jnp.int32)
    matches = species[:, None] == kinds[None, :]
    atom_scale = jnp.sum(jnp.where(matches, species_scale[None, :], 0.0), axis=1)
    atom_shift = jnp.sum(jnp.where(matches, species_shift[None, :], 0.0), axis=1)

    def block_step(totals, block_index):
        coord_grad, proj_grad = totals
        first_row = block_index * block_size
        center_block = lax.dynamic_slice_in_dim(center_proj, first_row, block_size, 0)
        neighbor_block = lax.dynamic_slice_in_dim(neighbor, first_row, block_size, 0)
        live_block = lax.dynamic_slice_in_dim(live_mask, first_row, block_size, 0)
        scale_block = lax.dynamic_slice_in_dim(atom_scale, first_row, block_size, 0)

        def energy_of(coords_all, proj_all, center_rows):
            return edge_sums(
                coords_all,
                proj_all,
                center_rows,
                first_row,
                neighbor_block,
                live_block,
                w_basis,
                w_env,
                w_latent,
                w_out,
                w_final,
            )

        sums, energy_back = jax.vjp(energy_of, all_coords, neighbor_proj, center_block)
        grad_coords, grad_proj, grad_center = energy_back(scale_block)
        return ((coord_grad + grad_coords, proj_grad + grad_proj), (sums, grad_center))

    start_totals = (
        jnp.zeros(all_coords.shape, jnp.float32),
        jnp.zeros(neighbor_proj.shape, jnp.float32),
    )
    (coord_grad, proj_grad), (sums, center_grad) = lax.scan(
        block_step, start_totals, jnp.arange(atom_count // block_size, dtype=jnp.int32)
    )
    atom_energy = atom_scale * sums.reshape(-1) + atom_shift
    (feature_grad,) = project_back((center_grad.reshape(atom_count, -1), proj_grad))
    return (
        atom_energy,
        coord_grad[:, :atom_count],
        coord_grad[:, atom_count:],
        feature_grad[:atom_count],
        feature_grad[atom_count:],
    )


def pass_x(payload, offset):
    return from_behind(payload, "gx", offset)


def pass_y(payload, offset):
    return from_behind(payload, "gy", offset)


def pass_z(payload, offset):
    return from_behind(payload, "gz", offset)


def half_x(payload, offset):
    return jax.tree.map(
        lambda part, own: part.astype(own.dtype),
        from_behind(for_sending(payload), "gx", offset),
        payload,
    )


def half_y(payload, offset):
    return jax.tree.map(
        lambda part, own: part.astype(own.dtype),
        from_behind(for_sending(payload), "gy", offset),
        payload,
    )


def half_z(payload, offset):
    return jax.tree.map(
        lambda part, own: part.astype(own.dtype),
        from_behind(for_sending(payload), "gz", offset),
        payload,
    )


def send_pair(passers, features_part, coords_part, offset):
    if passers[1] is None:
        return passers[0]((features_part, coords_part), offset)
    moved_coords = passers[0]((coords_part,), offset)[0]
    moved_features = passers[1]((features_part,), offset)[0]
    return (moved_features, moved_coords)


def carry_slab(passers, slab_features, slab_coords, offset):
    return send_pair(passers, slab_features, slab_coords, offset)


def section_x(features, coords, orient, forward):
    passers = (pass_x, half_x if forward else None)
    lower_part = carry_slab(passers, features[0], coords[:, 0], -orient)
    upper_part = carry_slab(passers, features[2], coords[:, 2], orient)
    return (
        jnp.stack([lower_part[0], features[1], upper_part[0]], axis=0),
        jnp.stack([lower_part[1], coords[:, 1], upper_part[1]], axis=1),
    )


def section_y(features, coords, orient, forward):
    passers = (pass_y, half_y if forward else None)
    lower_part = carry_slab(passers, features[:, 0], coords[:, :, 0], -orient)
    upper_part = carry_slab(passers, features[:, 2], coords[:, :, 2], orient)
    return (
        jnp.stack([lower_part[0], features[:, 1], upper_part[0]], axis=1),
        jnp.stack([lower_part[1], coords[:, :, 1], upper_part[1]], axis=2),
    )


def section_z(features, coords, orient, forward):
    passers = (pass_z, half_z if forward else None)
    lower_part = carry_slab(passers, features[:, :, 0], coords[:, :, :, 0], -orient)
    upper_part = carry_slab(passers, features[:, :, 2], coords[:, :, :, 2], orient)
    return (
        jnp.stack([lower_part[0], features[:, :, 1], upper_part[0]], axis=2),
        jnp.stack([lower_part[1], coords[:, :, :, 1], upper_part[1]], axis=3),
    )


def local(
    positions,
    atom_features,
    species,
    edge_neighbor,
    edge_live,
    send_list,
    species_scale,
    species_shift,
    w_center,
    w_neighbor,
    w_basis,
    w_env,
    w_latent,
    w_out,
    w_final,
):
    atom_count = positions.shape[1]
    ghost_width = send_list.shape[1]
    feature_width = atom_features.shape[1]
    depth_cells = atom_count // (SIDE * SIDE)
    flat_list = send_list.reshape(-1)
    features = (
        atom_features[flat_list].astype(jnp.bfloat16).reshape(3, 3, 3, ghost_width, feature_width)
    )
    coords = positions[:, flat_list].reshape(3, 3, 3, 3, ghost_width)
    features, coords = section_x(features, coords, 1, True)
    features, coords = section_y(features, coords, 1, True)
    features, coords = section_z(features, coords, 1, True)
    cell_index = jnp.arange(27, dtype=jnp.int32)
    travel = jnp.stack([cell_index // 9 - 1, cell_index // 3 % 3 - 1, cell_index % 3 - 1])
    cell_size = jnp.array([SIDE, SIDE, depth_cells], dtype=jnp.float32) * lattice_spacing
    shift_table = travel.astype(jnp.float32) * cell_size[:, None]
    ghost_coords = (coords.reshape(3, 27, ghost_width) - shift_table[:, :, None]).reshape(
        3, 27 * ghost_width
    )
    ghost_features = features.reshape(27 * ghost_width, feature_width)
    energy, own_cgrad, ghost_cgrad, own_fgrad, ghost_fgrad = local_terms(
        positions,
        atom_features,
        ghost_coords,
        ghost_features,
        species,
        edge_neighbor,
        edge_live,
        species_scale,
        species_shift,
        w_center,
        w_neighbor,
        w_basis,
        w_env,
        w_latent,
        w_out,
        w_final,
        BLK,
    )
    back_features = ghost_fgrad.reshape(3, 3, 3, ghost_width, feature_width)
    back_coords = ghost_cgrad.reshape(3, 3, 3, 3, ghost_width)
    back_features, back_coords = section_z(back_features, back_coords, -1, False)
    back_features, back_coords = section_y(back_features, back_coords, -1, False)
    back_features, back_coords = section_x(back_features, back_coords, -1, False)
    feature_total = own_fgrad.at[flat_list].add(
        back_features.reshape(27 * ghost_width, feature_width)
    )
    coord_total = own_cgrad.at[:, flat_list].add(back_coords.reshape(3, 27 * ghost_width))
    return (energy, -coord_total, feature_total)


def solution(mesh):
    placed = (
        P(None, ("gx", "gy", "gz")),
        P(("gx", "gy", "gz"), None),
        P(("gx", "gy", "gz")),
        P(("gx", "gy", "gz"), None),
        P(("gx", "gy", "gz"), None),
        P(("gx", "gy", "gz"), None),
        P(),
        P(),
        P(),
        P(),
        P(),
        P(),
        P(),
        P(),
        P(),
    )
    return jax.shard_map(
        local,
        mesh=mesh,
        in_specs=placed,
        out_specs=(P(("gx", "gy", "gz")), P(None, ("gx", "gy", "gz")), P(("gx", "gy", "gz"), None)),
        check_vma=False,
    )
```

profile of v0, /device:TPU:2, one launch (start us, length us, event | category | flops | bytes accessed | tf_op | source)
XLA Modules:
  0.0 1066.0 jit_solution(681028185135699478)
XLA Ops:
  2.9 2.6 gather_fusion.2
  6.4 3.7 gather_fusion.3
  13.8 2.7 collective-permute-start.3
  16.5 3.1 collective-permute-start.2
  22.8 3.5 collective-permute-start.4
  26.5 2.8 collective-permute-start.8
  32.4 8.1 collective-permute-done.8
  40.5 2.4 collective-permute-done.9
  43.1 2.7 collective-permute-start.10
  47.0 4.6 collective-permute-done.10
  51.6 4.5 collective-permute-done.11
  56.9 926.1 %while.19 = (s32[]{:T(128)}, f32[3,1360]{0,1:T(8,128)}, f32[1360,256]{1,0:T(8,128)S(1)}, f32[16,4]{1,0:T(8,128)}, bf16[16,4,256]{2,1,0:T(4,128)(2,1)}, /*index=5...) while((s32[]{:T(128)}, f32[3,1360]{0,1:T(8,128)}, ...), condition=%wide.region_28.29_spmd.clone, body=%wide.region_1.28_spmd.clone.sunk | while | flops 422942752 | bytes 46072392 | solution.py:191
  102.0 3.5 scatter_custom_fusion.11
  108.9 3.8 scatter_fusion
  159.7 3.5 scatter_custom_fusion.11
  166.8 3.8 scatter_fusion
  217.6 3.5 scatter_custom_fusion.11
  222.4 2.2 select_add_fusion.2
  224.7 3.8 scatter_fusion
  275.5 3.5 scatter_custom_fusion.11
  282.6 3.8 scatter_fusion
  333.3 3.5 scatter_custom_fusion.11
  338.2 2.2 select_add_fusion.2
  340.4 3.8 scatter_fusion
  391.2 3.5 scatter_custom_fusion.11
  396.1 2.2 select_add_fusion.2
  398.3 3.8 scatter_fusion
  449.1 3.5 scatter_custom_fusion.11
  453.9 2.2 select_add_fusion.2
  456.2 3.8 scatter_fusion
  507.0 3.5 scatter_custom_fusion.11
  514.0 3.8 scatter_fusion
  564.8 3.5 scatter_custom_fusion.11
  569.7 2.2 select_add_fusion.2
  571.9 3.8 scatter_fusion
  622.7 3.5 scatter_custom_fusion.11
  627.5 2.2 select_add_fusion.2
  629.8 3.8 scatter_fusion
  680.6 3.5 scatter_custom_fusion.11
  687.7 3.8 scatter_fusion
  738.5 3.5 scatter_custom_fusion.11
  743.3 2.2 select_add_fusion.2
  745.6 3.8 scatter_fusion
  796.3 3.5 scatter_custom_fusion.11
  801.2 2.2 select_add_fusion.2
  803.4 3.8 scatter_fusion
  854.2 3.5 scatter_custom_fusion.11
  859.1 2.2 select_add_fusion.2
  861.3 3.8 scatter_fusion
  912.1 3.5 scatter_custom_fusion.11
  916.9 2.2 select_add_fusion.2
  919.2 3.8 scatter_fusion
  970.0 3.5 scatter_custom_fusion.11
  974.8 2.2 select_add_fusion.2
  977.1 3.8 scatter_fusion
  988.1 2.4 collective-permute-start.19
  991.0 4.2 collective-permute-start.13
  995.9 14.4 %collective-permute-done.12 = f32[3,3,3,48]{3,2,1,0:T(4,128)S(1)} collective-permute-done((f32[3,3,3,48]{3,2,1,0:T(4,128)S(1)}, f32[3,3,3,48]{3,2,1,0:T(4,128)S(1)}, u32[]{:S(2)}, u32[]{:S(2)}) %collective-permute-start.12) | collective-permute-done | bytes 5216 | tf_op jit(solution)/shard_map/ppermute | solution.py:19
  1012.6 4.1 collective-permute-start.21
  1017.4 4.1 collective-permute-start.15
  1022.1 11.2 %collective-permute-done.14 = f32[3,3,3,48]{3,2,1,0:T(4,128)} collective-permute-done((f32[3,3,3,48]{3,2,1,0:T(4,128)}, f32[3,3,3,48]{3,2,1,0:T(4,128)}, u32[]{:S(2)}, u32[]{:S(2)}) %collective-permute-start.14) | collective-permute-done | bytes 5216 | tf_op jit(solution)/shard_map/ppermute | solution.py:19
  1040.9 4.1 collective-permute-done.16
  1045.4 9.0 scatter_fusion.1
  1056.2 9.1 scatter_fusion.2
  (3169 shorter events, 796.3 us)
Async XLA Ops:
  0.6 55.6 %copy-start = (bf16[256,256]{1,0:T(8,128)(2,1)S(1)}, bf16[256,256]{1,0:T(8,128)(2,1)}, u32[]{:S(2)}) copy-start(bf16[256,256]{1,0:T(8,128)(2,1)} %param.27) | copy-start | bytes 393220
  5.7 8.0 collective-permute-start
  5.9 7.8 collective-permute-start.1
  10.2 16.1 %collective-permute-start.6 = (bf16[3,3,48,256]{3,2,1,0:T(8,128)(2,1)S(1)}, bf16[3,3,48,256]{3,2,1,0:T(8,128)(2,1)S(1)}, u32[]{:S(2)}, u32[]{:S(2)}) collective-permute-start(bf16[3,3,48,256]{3,2,1,0:T(8,128)(2,1)S(1)} %bitcast.374), channel_id=1, source_target_pairs={{0,224},{32,0},{64,32},{96,64},{128,96},{160,128},{192,160},{224,1... | collective-permute-start | bytes 663560 | tf_op jit(solution)/shard_map/ppermute | solution.py:19
  12.1 14.2 %collective-permute-start.7 = (bf16[3,3,48,256]{3,2,1,0:T(8,128)(2,1)S(1)}, bf16[3,3,48,256]{3,2,1,0:T(8,128)(2,1)S(1)}, u32[]{:S(2)}, u32[]{:S(2)}) collective-permute-start(bf16[3,3,48,256]{3,2,1,0:T(8,128)(2,1)S(1)} %bitcast.372), channel_id=1, source_target_pairs={{0,32},{32,64},{64,96},{96,128},{128,160},{160,192},{192,224},{224... | collective-permute-start | bytes 663560 | tf_op jit(solution)/shard_map/ppermute | solution.py:19
  13.8 7.5 collective-permute-start.3
  16.5 6.2 collective-permute-start.2
  22.8 8.3 collective-permute-start.4
  26.3 5.9 collective-permute-start.5
  26.5 14.0 %collective-permute-start.8 = (bf16[3,3,48,256]{3,2,0,1:T(8,128)(2,1)S(1)}, bf16[3,3,48,256]{3,2,0,1:T(8,128)(2,1)S(1)}, u32[]{:S(2)}, u32[]{:S(2)}) collective-permute-start(bf16[3,3,48,256]{3,2,0,1:T(8,128)(2,1)S(1)} %get-tuple-element.475), channel_id=1, source_target_pairs={{0,24},{8,0},{16,8},{24,16},{1,25},{9,1},{17,9},{25,17},{2,26},{10... | collective-permute-start | bytes 663560 | tf_op jit(solution)/shard_map/ppermute | solution.py:19
  29.3 13.6 %collective-permute-start.9 = (bf16[3,3,48,256]{3,2,0,1:T(8,128)(2,1)S(1)}, bf16[3,3,48,256]{3,2,0,1:T(8,128)(2,1)S(1)}, u32[]{:S(2)}, u32[]{:S(2)}) collective-permute-start(bf16[3,3,48,256]{3,2,0,1:T(8,128)(2,1)S(1)} %get-tuple-element.476), channel_id=1, source_target_pairs={{0,8},{8,16},{16,24},{24,0},{1,9},{9,17},{17,25},{25,1},{2,10},{10... | collective-permute-start | bytes 663560 | tf_op jit(solution)/shard_map/ppermute | solution.py:19
  43.1 8.5 collective-permute-start.10
  45.8 10.3 collective-permute-start.11
  63.1 15.3 %copy-start.35 = (f32[4,128]{1,0:T(4,128)}, f32[4,128]{1,0:T(4,128)S(1)}, u32[]{:S(2)}) copy-start(f32[4,128]{1,0:T(4,128)S(1)} %get-tuple-element.652) | copy-start | bytes 6148 | tf_op jit(solution)/shard_map/while
  67.7 29.5 %copy-start.4 = (f32[512,256]{1,0:T(8,128)}, f32[512,256]{1,0:T(8,128)S(1)}, u32[]{:S(2)}) copy-start(f32[512,256]{1,0:T(8,128)S(1)} %fusion.190) | copy-start | bytes 1572868 | tf_op jit(solution)/shard_map/while
  114.6 10.8 %copy-start.56 = (f32[64]{0:T(128)}, f32[64]{0:T(128)S(1)}, u32[]{:S(2)}) copy-start(f32[64]{0:T(128)S(1)} %get-tuple-element.749) | copy-start | bytes 772 | tf_op jit(solution)/shard_map/while
  120.8 15.3 %copy-start.35 = (f32[4,128]{1,0:T(4,128)}, f32[4,128]{1,0:T(4,128)S(1)}, u32[]{:S(2)}) copy-start(f32[4,128]{1,0:T(4,128)S(1)} %get-tuple-element.652) | copy-start | bytes 6148 | tf_op jit(solution)/shard_map/while
  125.4 29.5 %copy-start.4 = (f32[512,256]{1,0:T(8,128)}, f32[512,256]{1,0:T(8,128)S(1)}, u32[]{:S(2)}) copy-start(f32[512,256]{1,0:T(8,128)S(1)} %fusion.190) | copy-start | bytes 1572868 | tf_op jit(solution)/shard_map/while
  178.7 15.3 %copy-start.35 = (f32[4,128]{1,0:T(4,128)}, f32[4,128]{1,0:T(4,128)S(1)}, u32[]{:S(2)}) copy-start(f32[4,128]{1,0:T(4,128)S(1)} %get-tuple-element.652) | copy-start | bytes 6148 | tf_op jit(solution)/shard_map/while
  183.2 29.5 %copy-start.4 = (f32[512,256]{1,0:T(8,128)}, f32[512,256]{1,0:T(8,128)S(1)}, u32[]{:S(2)}) copy-start(f32[512,256]{1,0:T(8,128)S(1)} %fusion.190) | copy-start | bytes 1572868 | tf_op jit(solution)/shard_map/while
  236.6 15.3 %copy-start.35 = (f32[4,128]{1,0:T(4,128)}, f32[4,128]{1,0:T(4,128)S(1)}, u32[]{:S(2)}) copy-start(f32[4,128]{1,0:T(4,128)S(1)} %get-tuple-element.652) | copy-start | bytes 6148 | tf_op jit(solution)/shard_map/while
  241.2 29.5 %copy-start.4 = (f32[512,256]{1,0:T(8,128)}, f32[512,256]{1,0:T(8,128)S(1)}, u32[]{:S(2)}) copy-start(f32[512,256]{1,0:T(8,128)S(1)} %fusion.190) | copy-start | bytes 1572868 | tf_op jit(solution)/shard_map/while
  288.3 10.8 %copy-start.56 = (f32[64]{0:T(128)}, f32[64]{0:T(128)S(1)}, u32[]{:S(2)}) copy-start(f32[64]{0:T(128)S(1)} %get-tuple-element.749) | copy-start | bytes 772 | tf_op jit(solution)/shard_map/while
  294.5 15.3 %copy-start.35 = (f32[4,128]{1,0:T(4,128)}, f32[4,128]{1,0:T(4,128)S(1)}, u32[]{:S(2)}) copy-start(f32[4,128]{1,0:T(4,128)S(1)} %get-tuple-element.652) | copy-start | bytes 6148 | tf_op jit(solution)/shard_map/while
  299.0 29.5 %copy-start.4 = (f32[512,256]{1,0:T(8,128)}, f32[512,256]{1,0:T(8,128)S(1)}, u32[]{:S(2)}) copy-start(f32[512,256]{1,0:T(8,128)S(1)} %fusion.190) | copy-start | bytes 1572868 | tf_op jit(solution)/shard_map/while
  346.1 10.8 %copy-start.56 = (f32[64]{0:T(128)}, f32[64]{0:T(128)S(1)}, u32[]{:S(2)}) copy-start(f32[64]{0:T(128)S(1)} %get-tuple-element.749) | copy-start | bytes 772 | tf_op jit(solution)/shard_map/while
  352.4 15.3 %copy-start.35 = (f32[4,128]{1,0:T(4,128)}, f32[4,128]{1,0:T(4,128)S(1)}, u32[]{:S(2)}) copy-start(f32[4,128]{1,0:T(4,128)S(1)} %get-tuple-element.652) | copy-start | bytes 6148 | tf_op jit(solution)/shard_map/while
  356.9 29.5 %copy-start.4 = (f32[512,256]{1,0:T(8,128)}, f32[512,256]{1,0:T(8,128)S(1)}, u32[]{:S(2)}) copy-start(f32[512,256]{1,0:T(8,128)S(1)} %fusion.190) | copy-start | bytes 1572868 | tf_op jit(solution)/shard_map/while
  410.3 15.3 %copy-start.35 = (f32[4,128]{1,0:T(4,128)}, f32[4,128]{1,0:T(4,128)S(1)}, u32[]{:S(2)}) copy-start(f32[4,128]{1,0:T(4,128)S(1)} %get-tuple-element.652) | copy-start | bytes 6148 | tf_op jit(solution)/shard_map/while
  414.8 29.5 %copy-start.4 = (f32[512,256]{1,0:T(8,128)}, f32[512,256]{1,0:T(8,128)S(1)}, u32[]{:S(2)}) copy-start(f32[512,256]{1,0:T(8,128)S(1)} %fusion.190) | copy-start | bytes 1572868 | tf_op jit(solution)/shard_map/while
  468.1 15.3 %copy-start.35 = (f32[4,128]{1,0:T(4,128)}, f32[4,128]{1,0:T(4,128)S(1)}, u32[]{:S(2)}) copy-start(f32[4,128]{1,0:T(4,128)S(1)} %get-tuple-element.652) | copy-start | bytes 6148 | tf_op jit(solution)/shard_map/while
  472.7 29.5 %copy-start.4 = (f32[512,256]{1,0:T(8,128)}, f32[512,256]{1,0:T(8,128)S(1)}, u32[]{:S(2)}) copy-start(f32[512,256]{1,0:T(8,128)S(1)} %fusion.190) | copy-start | bytes 1572868 | tf_op jit(solution)/shard_map/while
  526.0 15.3 %copy-start.35 = (f32[4,128]{1,0:T(4,128)}, f32[4,128]{1,0:T(4,128)S(1)}, u32[]{:S(2)}) copy-start(f32[4,128]{1,0:T(4,128)S(1)} %get-tuple-element.652) | copy-start | bytes 6148 | tf_op jit(solution)/shard_map/while
  530.5 29.5 %copy-start.4 = (f32[512,256]{1,0:T(8,128)}, f32[512,256]{1,0:T(8,128)S(1)}, u32[]{:S(2)}) copy-start(f32[512,256]{1,0:T(8,128)S(1)} %fusion.190) | copy-start | bytes 1572868 | tf_op jit(solution)/shard_map/while
  583.9 15.3 %copy-start.35 = (f32[4,128]{1,0:T(4,128)}, f32[4,128]{1,0:T(4,128)S(1)}, u32[]{:S(2)}) copy-start(f32[4,128]{1,0:T(4,128)S(1)} %get-tuple-element.652) | copy-start | bytes 6148 | tf_op jit(solution)/shard_map/while
  588.4 29.5 %copy-start.4 = (f32[512,256]{1,0:T(8,128)}, f32[512,256]{1,0:T(8,128)S(1)}, u32[]{:S(2)}) copy-start(f32[512,256]{1,0:T(8,128)S(1)} %fusion.190) | copy-start | bytes 1572868 | tf_op jit(solution)/shard_map/while
  641.7 15.3 %copy-start.35 = (f32[4,128]{1,0:T(4,128)}, f32[4,128]{1,0:T(4,128)S(1)}, u32[]{:S(2)}) copy-start(f32[4,128]{1,0:T(4,128)S(1)} %get-tuple-element.652) | copy-start | bytes 6148 | tf_op jit(solution)/shard_map/while
  646.3 29.5 %copy-start.4 = (f32[512,256]{1,0:T(8,128)}, f32[512,256]{1,0:T(8,128)S(1)}, u32[]{:S(2)}) copy-start(f32[512,256]{1,0:T(8,128)S(1)} %fusion.190) | copy-start | bytes 1572868 | tf_op jit(solution)/shard_map/while
  699.6 15.3 %copy-start.35 = (f32[4,128]{1,0:T(4,128)}, f32[4,128]{1,0:T(4,128)S(1)}, u32[]{:S(2)}) copy-start(f32[4,128]{1,0:T(4,128)S(1)} %get-tuple-element.652) | copy-start | bytes 6148 | tf_op jit(solution)/shard_map/while
  704.2 29.5 %copy-start.4 = (f32[512,256]{1,0:T(8,128)}, f32[512,256]{1,0:T(8,128)S(1)}, u32[]{:S(2)}) copy-start(f32[512,256]{1,0:T(8,128)S(1)} %fusion.190) | copy-start | bytes 1572868 | tf_op jit(solution)/shard_map/while
  751.3 10.8 %copy-start.56 = (f32[64]{0:T(128)}, f32[64]{0:T(128)S(1)}, u32[]{:S(2)}) copy-start(f32[64]{0:T(128)S(1)} %get-tuple-element.749) | copy-start | bytes 772 | tf_op jit(solution)/shard_map/while
  757.5 15.3 %copy-start.35 = (f32[4,128]{1,0:T(4,128)}, f32[4,128]{1,0:T(4,128)S(1)}, u32[]{:S(2)}) copy-start(f32[4,128]{1,0:T(4,128)S(1)} %get-tuple-element.652) | copy-start | bytes 6148 | tf_op jit(solution)/shard_map/while
  762.0 29.5 %copy-start.4 = (f32[512,256]{1,0:T(8,128)}, f32[512,256]{1,0:T(8,128)S(1)}, u32[]{:S(2)}) copy-start(f32[512,256]{1,0:T(8,128)S(1)} %fusion.190) | copy-start | bytes 1572868 | tf_op jit(solution)/shard_map/while
  809.1 10.8 %copy-start.56 = (f32[64]{0:T(128)}, f32[64]{0:T(128)S(1)}, u32[]{:S(2)}) copy-start(f32[64]{0:T(128)S(1)} %get-tuple-element.749) | copy-start | bytes 772 | tf_op jit(solution)/shard_map/while
  815.4 15.3 %copy-start.35 = (f32[4,128]{1,0:T(4,128)}, f32[4,128]{1,0:T(4,128)S(1)}, u32[]{:S(2)}) copy-start(f32[4,128]{1,0:T(4,128)S(1)} %get-tuple-element.652) | copy-start | bytes 6148 | tf_op jit(solution)/shard_map/while
  819.9 29.5 %copy-start.4 = (f32[512,256]{1,0:T(8,128)}, f32[512,256]{1,0:T(8,128)S(1)}, u32[]{:S(2)}) copy-start(f32[512,256]{1,0:T(8,128)S(1)} %fusion.190) | copy-start | bytes 1572868 | tf_op jit(solution)/shard_map/while
  873.3 15.3 %copy-start.35 = (f32[4,128]{1,0:T(4,128)}, f32[4,128]{1,0:T(4,128)S(1)}, u32[]{:S(2)}) copy-start(f32[4,128]{1,0:T(4,128)S(1)} %get-tuple-element.652) | copy-start | bytes 6148 | tf_op jit(solution)/shard_map/while
  877.8 29.5 %copy-start.4 = (f32[512,256]{1,0:T(8,128)}, f32[512,256]{1,0:T(8,128)S(1)}, u32[]{:S(2)}) copy-start(f32[512,256]{1,0:T(8,128)S(1)} %fusion.190) | copy-start | bytes 1572868 | tf_op jit(solution)/shard_map/while
  924.9 10.8 %copy-start.56 = (f32[64]{0:T(128)}, f32[64]{0:T(128)S(1)}, u32[]{:S(2)}) copy-start(f32[64]{0:T(128)S(1)} %get-tuple-element.749) | copy-start | bytes 772 | tf_op jit(solution)/shard_map/while
  931.1 15.3 %copy-start.35 = (f32[4,128]{1,0:T(4,128)}, f32[4,128]{1,0:T(4,128)S(1)}, u32[]{:S(2)}) copy-start(f32[4,128]{1,0:T(4,128)S(1)} %get-tuple-element.652) | copy-start | bytes 6148 | tf_op jit(solution)/shard_map/while
  935.7 29.5 %copy-start.4 = (f32[512,256]{1,0:T(8,128)}, f32[512,256]{1,0:T(8,128)S(1)}, u32[]{:S(2)}) copy-start(f32[512,256]{1,0:T(8,128)S(1)} %fusion.190) | copy-start | bytes 1572868 | tf_op jit(solution)/shard_map/while
  985.2 55.7 %copy-start.1 = (f32[1360,256]{1,0:T(8,128)}, f32[1360,256]{1,0:T(8,128)S(1)}, u32[]{:S(2)}) copy-start(f32[1360,256]{1,0:T(8,128)S(1)} %fusion.94) | copy-start | bytes 4177924
  986.4 24.0 %collective-permute-start.18 = (f32[3,3,48,256]{3,2,1,0:T(8,128)}, f32[3,3,48,256]{3,2,1,0:T(8,128)}, u32[]{:S(2)}, u32[]{:S(2)}) collective-permute-start(f32[3,3,48,256]{3,2,1,0:T(8,128)} %get-tuple-element.466), channel_id=1, source_target_pairs={{0,1},{1,2},{2,3},{3,4},{4,5},{5,6},{6,7},{7,0},{8,9},{9,10},{10,1... | collective-permute-start | bytes 1327112 | tf_op jit(solution)/shard_map/ppermute | solution.py:19
  988.1 22.3 %collective-permute-start.19 = (f32[3,3,48,256]{3,2,1,0:T(8,128)}, f32[3,3,48,256]{3,2,1,0:T(8,128)}, u32[]{:S(2)}, u32[]{:S(2)}) collective-permute-start(f32[3,3,48,256]{3,2,1,0:T(8,128)} %get-tuple-element.467), channel_id=1, source_target_pairs={{0,7},{1,0},{2,1},{3,2},{4,3},{5,4},{6,5},{7,6},{8,15},{9,8},{10,9... | collective-permute-start | bytes 1327112 | tf_op jit(solution)/shard_map/ppermute | solution.py:19
  990.7 19.5 %collective-permute-start.12 = (f32[3,3,3,48]{3,2,1,0:T(4,128)S(1)}, f32[3,3,3,48]{3,2,1,0:T(4,128)S(1)}, u32[]{:S(2)}, u32[]{:S(2)}) collective-permute-start(f32[3,3,3,48]{3,2,1,0:T(4,128)S(1)} %bitcast.397), channel_id=1, source_target_pairs={{0,1},{1,2},{2,3},{3,4},{4,5},{5,6},{6,7},{7,0},{8,9},{9,10},{10,1... | collective-permute-start | bytes 15560 | tf_op jit(solution)/shard_map/ppermute | solution.py:19
  991.0 19.3 %collective-permute-start.13 = (f32[3,3,3,48]{3,2,1,0:T(4,128)S(1)}, f32[3,3,3,48]{3,2,1,0:T(4,128)S(1)}, u32[]{:S(2)}, u32[]{:S(2)}) collective-permute-start(f32[3,3,3,48]{3,2,1,0:T(4,128)S(1)} %bitcast.398), channel_id=1, source_target_pairs={{0,7},{1,0},{2,1},{3,2},{4,3},{5,4},{6,5},{7,6},{8,15},{9,8},{10,9... | collective-permute-start | bytes 15560 | tf_op jit(solution)/shard_map/ppermute | solution.py:19
  1012.6 22.2 %collective-permute-start.20 = (f32[3,3,48,256]{3,2,0,1:T(8,128)}, f32[3,3,48,256]{3,2,0,1:T(8,128)S(1)}, u32[]{:S(2)}, u32[]{:S(2)}) collective-permute-start(f32[3,3,48,256]{3,2,0,1:T(8,128)} %get-tuple-element.463), channel_id=1, source_target_pairs={{0,8},{8,16},{16,24},{24,0},{1,9},{9,17},{17,25},{25,1},{2,10},{10... | collective-permute-start | bytes 1327112 | tf_op jit(solution)/shard_map/ppermute | solution.py:19
  1012.6 22.2 %collective-permute-start.21 = (f32[3,3,48,256]{3,2,0,1:T(8,128)S(1)}, f32[3,3,48,256]{3,2,0,1:T(8,128)}, u32[]{:S(2)}, u32[]{:S(2)}) collective-permute-start(f32[3,3,48,256]{3,2,0,1:T(8,128)S(1)} %get-tuple-element.464), channel_id=1, source_target_pairs={{0,24},{8,0},{16,8},{24,16},{1,25},{9,1},{17,9},{25,17},{2,26},{10... | collective-permute-start | bytes 1327112 | tf_op jit(solution)/shard_map/ppermute | solution.py:19
  1017.4 15.9 %collective-permute-start.14 = (f32[3,3,3,48]{3,2,1,0:T(4,128)}, f32[3,3,3,48]{3,2,1,0:T(4,128)}, u32[]{:S(2)}, u32[]{:S(2)}) collective-permute-start(f32[3,3,3,48]{3,2,1,0:T(4,128)} %get-tuple-element.487), channel_id=1, source_target_pairs={{0,8},{8,16},{16,24},{24,0},{1,9},{9,17},{17,25},{25,1},{2,10},{10... | collective-permute-start | bytes 15560 | tf_op jit(solution)/shard_map/ppermute | solution.py:19
  1017.4 16.6 %collective-permute-start.15 = (f32[3,3,3,48]{3,2,1,0:T(4,128)}, f32[3,3,3,48]{3,2,1,0:T(4,128)}, u32[]{:S(2)}, u32[]{:S(2)}) collective-permute-start(f32[3,3,3,48]{3,2,1,0:T(4,128)} %get-tuple-element.488), channel_id=1, source_target_pairs={{0,24},{8,0},{16,8},{24,16},{1,25},{9,1},{17,9},{25,17},{2,26},{10... | collective-permute-start | bytes 15560 | tf_op jit(solution)/shard_map/ppermute | solution.py:19
  1036.9 18.1 %collective-permute-start.22 = (f32[3,3,48,256]{3,2,1,0:T(8,128)}, f32[3,3,48,256]{3,2,1,0:T(8,128)S(1)}, u32[]{:S(2)}, u32[]{:S(2)}) collective-permute-start(f32[3,3,48,256]{3,2,1,0:T(8,128)} %get-tuple-element.460), channel_id=1, source_target_pairs={{0,32},{32,64},{64,96},{96,128},{128,160},{160,192},{192,224},{224... | collective-permute-start | bytes 1327112 | tf_op jit(solution)/shard_map/ppermute | solution.py:19
  1036.9 18.1 %collective-permute-start.23 = (f32[3,3,48,256]{3,2,1,0:T(8,128)S(1)}, f32[3,3,48,256]{3,2,1,0:T(8,128)}, u32[]{:S(2)}, u32[]{:S(2)}) collective-permute-start(f32[3,3,48,256]{3,2,1,0:T(8,128)S(1)} %get-tuple-element.461), channel_id=1, source_target_pairs={{0,224},{32,0},{64,32},{96,64},{128,96},{160,128},{192,160},{224,1... | collective-permute-start | bytes 1327112 | tf_op jit(solution)/shard_map/ppermute | solution.py:19
  1038.6 6.4 collective-permute-start.16
  1038.7 6.4 collective-permute-start.17
  (844 other events, 2127.4 us)
where the time goes:
time: 1080 us; the launch traced here: 1070 us
  other arithmetic  442 us (41%)
  local copies, waits for them, and re-layouts  372 us (34%)
  matrix products  133 us (12%)
  waiting for transfers between devices  54.2 us (5%)
  starting transfers between devices  39.1 us (4%)
  loops' own time  23.6 us (2%)
    while x1760, local copies, waits for them, and re-layouts  75.9 us
    scatter-add x16, other arithmetic, edge_sums(): jnp.take(neighbor_proj, flat_index, axis=0) + radial  60.9 us
    scatter-add x16, other arithmetic, edge_sums(): jnp.take(all_coords, flat_index, axis=1).reshape(3, block_size, slot_count)  55.7 us
    ppermute x24, waiting for transfers between devices, from_behind(): lax.ppermute(array, axis, [(i, (i + by) % size) for i in range(size)])  54.2 us
    gather x32, local copies, waits for them, and re-layouts, edge_sums(): jnp.take(all_coords, flat_index, axis=1).reshape(3, block_size, slot_count)  50.9 us
    another operation x48, other arithmetic  45 us
    ppermute x24, starting transfers between devices, from_behind(): lax.ppermute(array, axis, [(i, (i + by) % size) for i in range(size)])  39.1 us
    add x16, other arithmetic, block_step(): coord_grad + grad_coords  35.7 us
  transfers between devices with their start and end apart: 24, of which 11 were waited for; matrix products, arithmetic and copies ran while one was open for 2% of the time, Pallas kernels for 0%

commit v1 on v0

v1 whole, which is shorter than its diff:
```python
import functools
import math

import jax
import jax.numpy as jnp
from jax import lax
from jax.experimental import pallas as pl
from jax.experimental.pallas import tpu as pltpu
from jax.sharding import PartitionSpec as P

SIDE = 4
REACH = 3
SPACING = 2.15
CUT = 6.0
ENV_NORM = 0.125
ATOMS = 64
SLOTS = 128
GHOST = 48
WIDTH = 256
CHANNELS = 64
OUT_WIDTH = 128
BASIS = 8
LIST = 1024
HEAD = 896
BASIS_AT = 1000
CENTER_AT = 1008
GROUP = 8
MESSAGE = 64

f32 = jnp.float32
bf16 = jnp.bfloat16
i32 = jnp.int32

DIRECTIONS = [
    (tx, ty, tz)
    for tx in (-1, 0, 1)
    for ty in (-1, 0, 1)
    for tz in (-1, 0, 1)
    if (tx, ty, tz) != (0, 0, 0)
]
CELLS = [9 * (tx + 1) + 3 * (ty + 1) + tz + 1 for tx, ty, tz in DIRECTIONS]
SIZES = [math.prod(REACH if t else SIDE for t in d) for d in DIRECTIONS]
STARTS = [ATOMS + sum(SIZES[:i]) for i in range(26)]
assert STARTS[-1] + SIZES[-1] == BASIS_AT


def nn(a, b):
    return jnp.dot(a, b, preferred_element_type=f32)


def nt(a, b):
    return lax.dot_general(a, b, (((1,), (1,)), ((), ())), preferred_element_type=f32)


def lanes_of(shape):
    return lax.broadcasted_iota(i32, shape, len(shape) - 1)


def rows_of(shape):
    return lax.broadcasted_iota(i32, shape, 0)


def column(row, size):
    shape = (size, size)
    on = rows_of(shape) == lanes_of(shape)
    return jnp.sum(jnp.where(on, jnp.broadcast_to(row, shape), 0.0), axis=1, keepdims=True)


def row(col, size):
    shape = (size, size)
    on = rows_of(shape) == lanes_of(shape)
    return jnp.sum(jnp.where(on, jnp.broadcast_to(col, shape), 0.0), axis=0, keepdims=True)


def pieces(value):
    high = value.astype(bf16).astype(f32)
    rest = value - high
    middle = rest.astype(bf16).astype(f32)
    low = (rest - middle).astype(bf16).astype(f32)
    return high, middle, low


def sigmoid(x):
    return 0.5 * jnp.tanh(0.5 * x) + 0.5


def pack_kernel(features, positions, lists, w_center, w_neighbor, message, proj, center, square, held):
    rounded = features[...].astype(bf16)
    own = nn(rounded, w_neighbor[...]).astype(bf16)
    proj[...] = own
    center[...] = nn(rounded, w_center[...]).astype(bf16)
    square[...] = jnp.zeros((128, 128), f32)
    square[0:3, 0:ATOMS] = positions[...]
    high, middle, low = pieces(square[0:8, :])
    parts = jnp.concatenate([high, middle, low, jnp.zeros((8, 128), f32)], axis=0).astype(bf16)
    held[0:ATOMS, :] = own
    held[ATOMS:128, :] = jnp.zeros((128 - ATOMS, WIDTH), bf16)
    square[0:27, 0:GHOST] = lists[...].astype(f32)
    by_entry = square[...].T
    wide = lanes_of((128, 128)).astype(f32)
    for i, cell in enumerate(CELLS):
        chosen = jnp.where(by_entry[:, cell : cell + 1] == wide, 1.0, 0.0).astype(bf16)
        message[i, 0:GHOST, :] = nn(chosen[0:GHOST], held[...]).astype(bf16)
        moved = nt(parts, chosen)
        message[i, GHOST:MESSAGE, :] = jnp.concatenate([moved[0:16], moved[16:32]], axis=1).astype(bf16)


def pack(features, positions, lists, w_center, w_neighbor):
    return pl.pallas_call(
        pack_kernel,
        out_shape=(
            jax.ShapeDtypeStruct((26, MESSAGE, WIDTH), bf16),
            jax.ShapeDtypeStruct((ATOMS, WIDTH), bf16),
            jax.ShapeDtypeStruct((ATOMS, WIDTH), bf16),
        ),
        in_specs=[pl.BlockSpec(memory_space=pltpu.VMEM)] * 5,
        out_specs=(pl.BlockSpec(memory_space=pltpu.VMEM),) * 3,
        scratch_shapes=[pltpu.VMEM((128, 128), f32), pltpu.VMEM((128, WIDTH), bf16)],
        name="pack",
    )(features, positions, lists, w_center, w_neighbor)


def exchange_kernel(sizes, sign, source, target, send_sem, recv_sem):
    axes = ("gx", "gy", "gz")
    here = [lax.axis_index(a) for a in axes]

    def place(direction):
        return tuple(
            lax.rem(h + (sign * t + n), n) for h, t, n in zip(here, direction, sizes)
        )

    barrier = pltpu.get_barrier_semaphore()
    for d in DIRECTIONS:
        pl.semaphore_signal(barrier, inc=1, device_id=place(d), device_id_type=pl.DeviceIdType.MESH)
    pl.semaphore_wait(barrier, 26)
    copies = []
    for i, d in enumerate(DIRECTIONS):
        copy = pltpu.make_async_remote_copy(
            src_ref=source.at[i],
            dst_ref=target.at[i],
            send_sem=send_sem.at[i],
            recv_sem=recv_sem.at[i],
            device_id=place(d),
            device_id_type=pl.DeviceIdType.MESH,
        )
        copy.start()
        copies.append(copy)
    for copy in copies:
        copy.wait()


def exchange(message, sizes, sign):
    return pl.pallas_call(
        functools.partial(exchange_kernel, sizes, sign),
        out_shape=jax.ShapeDtypeStruct(message.shape, message.dtype),
        in_specs=[pl.BlockSpec(memory_space=pl.ANY)],
        out_specs=pl.BlockSpec(memory_space=pl.ANY),
        scratch_shapes=[pltpu.SemaphoreType.DMA((26,)), pltpu.SemaphoreType.DMA((26,))],
        compiler_params=pltpu.CompilerParams(
            collective_id=0 if sign > 0 else 1, has_side_effects=True
        ),
        name="exchange_out" if sign > 0 else "exchange_back",
    )(message)


R_INDEX, R_ENV, R_SCALED, R_SCALE, R_SLOPE, R_U, R_INV, R_Y, R_BESS, R_BESS_D = 0, 1, 2, 3, 4, 5, 8, 9, 17, 25
R_COUNT = 33


def geometry(index, rx, ry, rz, live, scale):
    squared = rx * rx + ry * ry + rz * rz
    distance = jnp.sqrt(squared)
    inverse = 1.0 / distance
    ux, uy, uz = rx * inverse, ry * inverse, rz * inverse
    x = distance * (1.0 / CUT)
    x2 = x * x
    x5 = x2 * x2 * x
    x6 = x5 * x
    inside = jnp.where(x < 1.0, live, 0.0)
    env = inside * (1.0 + x6 * (-28.0 + x * (48.0 - 21.0 * x)))
    slope = inside * (x5 * (-168.0 + x * (336.0 - 168.0 * x))) * (1.0 / CUT)
    s3, s5, s15 = math.sqrt(3.0), math.sqrt(5.0), math.sqrt(15.0)
    ys = [
        s3 * ux,
        s3 * uy,
        s3 * uz,
        s15 * ux * uy,
        s15 * uy * uz,
        0.5 * s5 * (3.0 * uz * uz - 1.0),
        s15 * ux * uz,
        0.5 * s15 * (ux * ux - uy * uy),
    ]
    theta = distance * (math.pi / CUT)
    sin1, cos1 = jnp.sin(theta), jnp.cos(theta)
    sines, cosines = [jnp.zeros_like(sin1), sin1], [jnp.ones_like(cos1), cos1]
    for _ in range(BASIS - 1):
        sines.append(2.0 * cos1 * sines[-1] - sines[-2])
        cosines.append(2.0 * cos1 * cosines[-1] - cosines[-2])
    norm = math.sqrt(2.0 / CUT)
    bess, bess_d = [], []
    for n in range(1, BASIS + 1):
        value = norm * sines[n] * inverse
        bess.append(value)
        bess_d.append((norm * n * math.pi / CUT * cosines[n] - value) * inverse)
    return [index, env, env * scale, scale, slope, ux, uy, uz, inverse] + ys + bess + bess_d


def edge_blocks(
    per_atom,
    slots,
    table,
    onehot,
    head_proj,
    tail_proj,
    w_env,
    w_latent,
    w_out,
    w_basis,
    env_t,
    latent_t,
    out_t,
    final_col,
    acc,
    acc_tail,
    energy,
):
    width = GROUP * per_atom
    lane = lanes_of((GROUP, 128))

    def chunks_of(q):
        atoms = [slots[q, pl.ds(j, GROUP, stride=GROUP), :] for j in range(GROUP)]
        if per_atom == SLOTS:
            return atoms
        out = []
        for g in (0, 4):
            a0 = atoms[g]
            a1 = pltpu.roll(atoms[g + 1], 96, 1)
            a2 = pltpu.roll(atoms[g + 2], 64, 1)
            a3 = pltpu.roll(atoms[g + 3], 32, 1)
            out += [
                jnp.where(lane < 96, a0, a1),
                jnp.where(lane < 64, a1, a2),
                jnp.where(lane < 32, a2, a3),
            ]
        return out

    packed = [jnp.concatenate(chunks_of(q), axis=1) for q in range(6)]
    for q, value in enumerate(geometry(*packed)):
        for k in range(width // 128):
            table[k, q * GROUP : (q + 1) * GROUP, :] = value[:, 128 * k : 128 * k + 128]

    acc[...] = jnp.zeros(acc.shape, f32)

    wide = (GROUP, width)
    first_lane = rows_of(wide) * per_atom
    mask = (lanes_of(wide) >= first_lane) & (lanes_of(wide) < first_lane + per_atom)
    maskf = jnp.where(mask, 1.0, 0.0).astype(f32)

    deg = rows_of((3 * CHANNELS, 80)) // CHANNELS
    comp = lanes_of((3 * CHANNELS, 80)) // GROUP
    allowed = (
        ((deg == 0) & (comp == 0))
        | ((deg == 1) & (comp >= 1) & (comp <= 3))
        | ((deg == 2) & (comp >= 4) & (comp <= 8))
    )

    def block(b, carry):
        def value(q):
            parts = [table[k, pl.ds(q * GROUP + b, 1), :] for k in range(width // 128)]
            return jnp.concatenate(parts, axis=1)

        def eight(q):
            place = pl.ds(q * GROUP + b, GROUP, stride=GROUP)
            return jnp.concatenate([table[k, place, :] for k in range(width // 128)], axis=1)

        index = value(R_INDEX).astype(i32)
        env = value(R_ENV)
        bess = eight(R_BESS)
        tile = (16, width)
        apart = (jnp.broadcast_to(index, tile) - rows_of(tile)).astype(jnp.int16)
        for h in range(BASIS_AT // 16):
            onehot[16 * h : 16 * h + 16, 0:width] = jnp.where(
                apart == jnp.int16(16 * h), jnp.ones(tile, bf16), jnp.zeros(tile, bf16)
            )
        last = jnp.where(index == rows_of(wide) + (BASIS_AT - 8), 1.0, 0.0)
        onehot[BASIS_AT - 8 : BASIS_AT + 8, 0:width] = jnp.concatenate([last, bess], axis=0).astype(bf16)
        onehot[CENTER_AT:LIST, 0:width] = jnp.concatenate(
            [maskf, jnp.zeros(wide, f32)], axis=0
        ).astype(bf16)
        hot = onehot[:, 0:width]

        pre = nn(jnp.concatenate([head_proj[...], tail_proj[b]], axis=1), hot)
        sig = sigmoid(pre)
        act = pre * sig
        act_d = sig + act * (1.0 - sig)
        latent = env * act
        latent_h = latent.astype(bf16)
        weights = nn(env_t[...], latent_h)
        weights_h = weights.astype(bf16)
        ys = eight(R_Y)
        harm = jnp.concatenate(
            [maskf]
            + [maskf * ys[m : m + 1] for m in range(8)]
            + [jnp.zeros(wide, f32)],
            axis=0,
        ).astype(bf16)
        around = jnp.where(allowed, ENV_NORM * nt(weights_h, harm), 0.0)
        around_h = around.astype(bf16)
        tensor = nn(around_h, harm)
        scalars_h = (weights * tensor).astype(bf16)
        mixed = nn(latent_t[...], jnp.concatenate([latent_h, scalars_h], axis=0))
        sig = sigmoid(mixed)
        update = mixed * sig
        update_d = sig + update * (1.0 - sig)
        refined_h = (latent + env * update).astype(bf16)
        hidden = nn(out_t[...], refined_h)
        sig = sigmoid(hidden)
        hidden_act = hidden * sig
        final = final_col[:, 0:1]
        per_edge = jnp.sum(hidden_act * final, axis=0, keepdims=True)
        energy[pl.ds(pl.multiple_of(b * GROUP, GROUP), GROUP), :] = jnp.broadcast_to(
            jnp.sum(maskf * (env * per_edge), axis=1, keepdims=True), (GROUP, 128)
        )

        scaled = value(R_SCALED)
        d_hidden = ((sig + hidden_act * (1.0 - sig)) * final * scaled).astype(bf16)
        d_refined = nn(w_out[...], d_hidden)
        d_env = value(R_SCALE) * per_edge
        d_env += jnp.sum(d_refined * update, axis=0, keepdims=True)
        d_mixed = (env * d_refined * update_d).astype(bf16)
        d_both = nn(w_latent[...], d_mixed)
        d_scalars = d_both[WIDTH:]
        d_tensor_h = (d_scalars * weights).astype(bf16)
        d_around = jnp.where(allowed, ENV_NORM * nt(d_tensor_h, harm), 0.0)
        d_weights = d_scalars * tensor + nn(d_around.astype(bf16), harm)
        d_latent = d_refined + d_both[0:WIDTH] + nn(w_env[...], d_weights.astype(bf16))
        d_env += jnp.sum(d_latent * act, axis=0, keepdims=True)
        d_pre = (env * d_latent * act_d).astype(bf16)
        d_bess = nn(w_basis[...], d_pre)
        both = jnp.concatenate([around.T, d_around.T], axis=1).astype(bf16)
        d_harm = nn(both, jnp.concatenate([d_tensor_h, weights_h], axis=0))
        dy = [
            jnp.sum(maskf * d_harm[m * GROUP : (m + 1) * GROUP], axis=0, keepdims=True)
            for m in range(1, 9)
        ]

        ux, uy, uz, inverse = (value(q) for q in (R_U, R_U + 1, R_U + 2, R_INV))
        d_dist = d_env * value(R_SLOPE) + jnp.sum(d_bess * eight(R_BESS_D), axis=0, keepdims=True)
        s3, s5, s15 = math.sqrt(3.0), math.sqrt(5.0), math.sqrt(15.0)
        gx = s3 * dy[0] + s15 * (uy * dy[3] + uz * dy[6] + ux * dy[7])
        gy = s3 * dy[1] + s15 * (ux * dy[3] + uz * dy[4] - uy * dy[7])
        gz = s3 * dy[2] + s15 * (uy * dy[4] + ux * dy[6]) + 3.0 * s5 * uz * dy[5]
        along = d_dist - inverse * (gx * ux + gy * uy + gz * uz)
        d_rel = [inverse * g + along * u for g, u in ((gx, ux), (gy, uy), (gz, uz))]
        place = rows_of(wide)
        moved = jnp.where(place == 0, d_rel[0], 0.0)
        moved = jnp.where(place == 1, d_rel[1], moved)
        moved = jnp.where(place == 2, d_rel[2], moved)
        high = moved.astype(bf16).astype(f32)
        moved_h = jnp.concatenate([high, moved - high], axis=0).astype(bf16)
        spread = nt(jnp.concatenate([d_pre, moved_h], axis=0), hot)
        acc[...] += spread[:, 0:HEAD]
        acc_tail[b] = spread[:, HEAD:]
        return carry

    lax.fori_loop(0, ATOMS // GROUP, block, 0)


def edge_kernel(
    received,
    proj,
    center,
    positions,
    species,
    neighbor,
    live_in,
    kind_scale,
    kind_shift,
    w_basis,
    w_env,
    w_latent,
    w_out,
    w_final,
    energy_out,
    back,
    own_proj_grad,
    center_grad,
    own_pos_grad,
    rows,
    tail_rows,
    coords,
    head_proj,
    tail_proj,
    env_t,
    latent_t,
    out_t,
    final_col,
    slots,
    table,
    onehot,
    acc,
    acc_tail,
    energy,
):
    rows[0:ATOMS, :] = proj[...].astype(f32)
    for i in range(26):
        rows[STARTS[i] : STARTS[i] + SIZES[i], :] = received[i, 0:GHOST, :].astype(f32)[0 : SIZES[i]]
    rows[BASIS_AT:CENTER_AT, :] = w_basis[...].astype(f32)
    rows[CENTER_AT:LIST, :] = jnp.zeros((LIST - CENTER_AT, WIDTH), f32)
    for k in range(HEAD // 128):
        head_proj[:, 128 * k : 128 * k + 128] = rows[128 * k : 128 * k + 128, :].T.astype(bf16)
    for b in range(ATOMS // GROUP):
        rows[CENTER_AT : CENTER_AT + GROUP, :] = center[...].astype(f32)[GROUP * b : GROUP * b + GROUP]
        tail_proj[b] = rows[HEAD:LIST, :].T.astype(bf16)

    lane = lanes_of((8, 128))
    coords[...] = jnp.zeros(coords.shape, f32)
    coords[0:3, 0:ATOMS] = positions[...]
    filled = [coords[0:8, 128 * k : 128 * k + 128] for k in range(8)]
    which = rows_of((8, 128))
    for i, d in enumerate(DIRECTIONS):
        block = received[i, GHOST:MESSAGE, :].astype(f32)
        value = block[0:8, 0:128] + block[8:16, 0:128] + block[0:8, 128:256]
        step = [t * SIDE * SPACING for t in d]
        shift = jnp.where(which == 0, step[0], jnp.where(which == 1, step[1], step[2]))
        value = value - shift
        k, at = divmod(STARTS[i], 128)
        end = at + SIZES[i]
        value = pltpu.roll(value, at, 1) if at else value
        filled[k] = jnp.where((lane >= at) & (lane < end), value, filled[k])
        if end > 128:
            filled[k + 1] = jnp.where(lane < end - 128, value, filled[k + 1])

    env_t[...] = w_env[...].astype(f32).T.astype(bf16)
    latent_t[...] = w_latent[...].astype(f32).T.astype(bf16)
    out_t[...] = w_out[...].astype(f32).T.astype(bf16)
    final_col[...] = jnp.broadcast_to(column(w_final[...], OUT_WIDTH), (OUT_WIDTH, 128))

    kinds = species[...]
    scale_row = jnp.where(
        kinds == 0,
        kind_scale[0],
        jnp.where(kinds == 1, kind_scale[1], jnp.where(kinds == 2, kind_scale[2], kind_scale[3])),
    )
    shift_row = jnp.where(
        kinds == 0,
        kind_shift[0],
        jnp.where(kinds == 1, kind_shift[1], jnp.where(kinds == 2, kind_shift[2], kind_shift[3])),
    )

    full = (ATOMS, SLOTS)
    local = neighbor[...]
    ghost = local - ATOMS
    cell = jnp.where(ghost < 0, 13, (ghost * 1366) >> 16)
    jump = jnp.zeros((8, 128), i32)
    for i, c in enumerate(CELLS):
        jump = jnp.where(lane == c, STARTS[i] - ATOMS - GHOST * c, jump)
    jump = jnp.concatenate([jump] * 8, axis=0)
    index = local + jnp.take_along_axis(jump, cell, axis=1, mode="promise_in_bounds")
    low, page = index & 127, index >> 7
    rel = []
    for a in range(3):
        found = jnp.zeros(full, f32)
        for k in range(8):
            source = jnp.broadcast_to(filled[k][a : a + 1, :], full)
            taken = jnp.take_along_axis(source, low, axis=1, mode="promise_in_bounds")
            found = jnp.where(page == k, taken, found)
        rel.append(found - column(positions[a : a + 1, :], ATOMS))
    distance = jnp.sqrt(rel[0] * rel[0] + rel[1] * rel[1] + rel[2] * rel[2])
    live = jnp.where(distance * (1.0 / CUT) < 1.0, live_in[...], 0)

    before = jnp.where(rows_of((SLOTS, SLOTS)) < lanes_of((SLOTS, SLOTS)), 1.0, 0.0).astype(bf16)
    gap = nn((1 - live).astype(f32).astype(bf16), before).astype(i32)
    most = jnp.max(jnp.sum(live.astype(f32), axis=1, keepdims=True))
    values = [index] + rel
    for step in range(7):
        by = 1 << step
        moves = jnp.where((gap & by) != 0, live, 0)
        come = pltpu.roll(moves, SLOTS - by, 1) != 0
        values = [jnp.where(come, pltpu.roll(v, SLOTS - by, 1), v) for v in values]
        gap = jnp.where(come, pltpu.roll(gap, SLOTS - by, 1), gap)
        live = jnp.where(come, 1, live - moves)
    kept = live != 0
    slots[0] = jnp.where(kept, values[0], LIST - 1).astype(f32)
    slots[1] = jnp.where(kept, values[1], 0.5 * CUT)
    slots[2] = jnp.where(kept, values[2], 0.0)
    slots[3] = jnp.where(kept, values[3], 0.0)
    slots[4] = live.astype(f32)
    slots[5] = jnp.broadcast_to(column(scale_row, ATOMS), full)

    shared = (
        slots,
        table,
        onehot,
        head_proj,
        tail_proj,
        w_env,
        w_latent,
        w_out,
        w_basis,
        env_t,
        latent_t,
        out_t,
        final_col,
        acc,
        acc_tail,
        energy,
    )

    @pl.when(most <= 96.0)
    def _():
        edge_blocks(96, *shared)

    @pl.when(most > 96.0)
    def _():
        edge_blocks(SLOTS, *shared)

    energy_out[...] = scale_row * row(energy[:, 0:1], ATOMS) + shift_row

    tail = acc_tail[0]
    for b in range(1, ATOMS // GROUP):
        tail = tail + acc_tail[b]
    for k in range(HEAD // 128):
        rows[128 * k : 128 * k + 128, :] = acc[0:WIDTH, 128 * k : 128 * k + 128].T
    rows[HEAD:LIST, :] = tail[0:WIDTH].T
    place = CENTER_AT - HEAD
    pulled = jnp.zeros((8, 128), f32)
    for b in range(ATOMS // GROUP):
        tail_rows[...] = acc_tail[b][0:WIDTH].T
        center_grad[GROUP * b : GROUP * b + GROUP, :] = tail_rows[place : place + GROUP, :]
        value = acc_tail[b][WIDTH : WIDTH + 8] + acc_tail[b][WIDTH + 8 : WIDTH + 16]
        value = pltpu.roll(value, (GROUP * b - place) % 128, 1)
        pulled = jnp.where((lane >= GROUP * b) & (lane < GROUP * b + GROUP), value, pulled)
    coord_grad = [
        acc[WIDTH : WIDTH + 8, 128 * k : 128 * k + 128] + acc[WIDTH + 8 : WIDTH + 16, 128 * k : 128 * k + 128]
        for k in range(HEAD // 128)
    ]
    coord_grad.append(tail[WIDTH : WIDTH + 8] + tail[WIDTH + 8 : WIDTH + 16])
    own_proj_grad[...] = rows[0:ATOMS, :]
    own_pos_grad[...] = jnp.where(lane < ATOMS, coord_grad[0] - pulled, 0.0)
    entry = rows_of((GHOST, WIDTH))
    for i in range(26):
        value = rows[STARTS[i] : STARTS[i] + GHOST, :] if STARTS[i] + GHOST <= LIST else None
        if value is None:
            tail_rows[0:GHOST, :] = jnp.zeros((GHOST, WIDTH), f32)
            tail_rows[0 : SIZES[i], :] = rows[STARTS[i] : STARTS[i] + SIZES[i], :]
            value = tail_rows[0:GHOST, :]
        elif SIZES[i] < GHOST:
            value = jnp.where(entry < SIZES[i], value, 0.0)
        back[i, 0:GHOST, :] = value.astype(bf16)
        k, at = divmod(STARTS[i], 128)
        moved = coord_grad[k]
        if at:
            moved = pltpu.roll(moved, 128 - at, 1)
        if at + SIZES[i] > 128:
            moved = jnp.where(lane < 128 - at, moved, pltpu.roll(coord_grad[k + 1], 128 - at, 1))
        moved = jnp.where(lane < SIZES[i], moved, 0.0)
        high, middle, lowest = pieces(moved)
        back[i, GHOST:MESSAGE, :] = jnp.concatenate(
            [
                jnp.concatenate([high, middle], axis=0),
                jnp.concatenate([lowest, jnp.zeros((8, 128), f32)], axis=0),
            ],
            axis=1,
        ).astype(bf16)


def edges(received, proj, center, positions, species, neighbor, live, scale, shift, *weights):
    vmem = pl.BlockSpec(memory_space=pltpu.VMEM)
    smem = pl.BlockSpec(memory_space=pltpu.SMEM)
    return pl.pallas_call(
        edge_kernel,
        out_shape=(
            jax.ShapeDtypeStruct((1, ATOMS), f32),
            jax.ShapeDtypeStruct((26, MESSAGE, WIDTH), bf16),
            jax.ShapeDtypeStruct((ATOMS, WIDTH), f32),
            jax.ShapeDtypeStruct((ATOMS, WIDTH), f32),
            jax.ShapeDtypeStruct((8, 128), f32),
        ),
        in_specs=[vmem] * 7 + [smem] * 2 + [vmem] * 5,
        out_specs=(vmem,) * 5,
        scratch_shapes=[
            pltpu.VMEM((LIST, WIDTH), f32),
            pltpu.VMEM((128, WIDTH), f32),
            pltpu.VMEM((8, LIST), f32),
            pltpu.VMEM((WIDTH, HEAD), bf16),
            pltpu.VMEM((8, WIDTH, 128), bf16),
            pltpu.VMEM((3 * CHANNELS, WIDTH), bf16),
            pltpu.VMEM((WIDTH, WIDTH + 3 * CHANNELS), bf16),
            pltpu.VMEM((OUT_WIDTH, WIDTH), bf16),
            pltpu.VMEM((OUT_WIDTH, 128), f32),
            pltpu.VMEM((6, ATOMS, SLOTS), f32),
            pltpu.VMEM((8, R_COUNT * GROUP, 128), f32),
            pltpu.VMEM((LIST, GROUP * SLOTS), bf16),
            pltpu.VMEM((WIDTH + 16, HEAD), f32),
            pltpu.VMEM((8, WIDTH + 16, 128), f32),
            pltpu.VMEM((ATOMS, 128), f32),
        ],
        compiler_params=pltpu.CompilerParams(vmem_limit_bytes=56 * 1024 * 1024),
        name="edges",
    )(received, proj, center, positions, species, neighbor, live, scale, shift, *weights)


def unpack_kernel(
    returned, own_proj_grad, center_grad, own_pos_grad, lists, w_center, w_neighbor, forces, feature_grad, padded
):
    padded[...] = jnp.full((32, 128), -1, i32)
    padded[0:27, 0:GHOST] = lists[...]
    proj_grad = own_proj_grad[...]
    pos_grad = jnp.zeros((32, ATOMS), f32)
    atom = rows_of((ATOMS, GHOST))
    for i, cell in enumerate(CELLS):
        chosen = jnp.where(padded[cell : cell + 1, 0:GHOST] == atom, 1.0, 0.0).astype(bf16)
        proj_grad = proj_grad + nn(chosen, returned[i, 0:GHOST, :])
        block = returned[i, GHOST:MESSAGE, :]
        parts = jnp.concatenate([block[:, 0:GHOST], block[:, 128 : 128 + GHOST]], axis=0)
        pos_grad = pos_grad + nt(parts, chosen)
    feature_grad[...] = nt(proj_grad.astype(bf16), w_neighbor[...]) + nt(
        center_grad[...].astype(bf16), w_center[...]
    )
    total = own_pos_grad[:, 0:ATOMS] + pos_grad[0:8] + pos_grad[8:16] + pos_grad[16:24]
    forces[...] = -total[0:3]


def unpack(*args):
    vmem = pl.BlockSpec(memory_space=pltpu.VMEM)
    return pl.pallas_call(
        unpack_kernel,
        out_shape=(
            jax.ShapeDtypeStruct((3, ATOMS), f32),
            jax.ShapeDtypeStruct((ATOMS, WIDTH), f32),
        ),
        in_specs=[vmem] * 7,
        out_specs=(vmem,) * 2,
        scratch_shapes=[pltpu.VMEM((32, 128), i32)],
        name="unpack",
    )(*args)


def solution(mesh):
    sizes = tuple(mesh.shape[a] for a in ("gx", "gy", "gz"))

    def local(
        positions,
        atom_features,
        species,
        edge_neighbor,
        edge_live,
        send_list,
        species_scale,
        species_shift,
        w_center,
        w_neighbor,
        w_basis,
        w_env,
        w_latent,
        w_out,
        w_final,
    ):
        message, proj, center = pack(atom_features, positions, send_list, w_center, w_neighbor)
        received = exchange(message, sizes, 1)
        energy, back, own_proj_grad, center_grad, own_pos_grad = edges(
            received,
            proj,
            center,
            positions,
            species.reshape(1, ATOMS),
            edge_neighbor,
            edge_live,
            species_scale,
            species_shift,
            w_basis,
            w_env,
            w_latent,
            w_out,
            w_final.reshape(1, OUT_WIDTH),
        )
        returned = exchange(back, sizes, -1)
        forces, feature_grad = unpack(
            returned, own_proj_grad, center_grad, own_pos_grad, send_list, w_center, w_neighbor
        )
        return energy.reshape(ATOMS), forces, feature_grad

    split = ("gx", "gy", "gz")
    return jax.shard_map(
        local,
        mesh=mesh,
        in_specs=(P(None, split), P(split, None), P(split), P(split, None), P(split, None), P(split, None))
        + (P(),) * 9,
        out_specs=(P(split), P(None, split), P(split, None)),
        check_vma=False,
    )
```

time: 1080 us -> 96.3 us (0.09); the launches traced: 1070 us -> 94.8 us
  other arithmetic: 442 us -> 0 us
  local copies, waits for them, and re-layouts: 372 us -> 1.65 us
  matrix products: 133 us -> 0 us
  Pallas kernels: 0 us -> 92.5 us
  waiting for transfers between devices: 54.2 us -> 0 us
  starting transfers between devices: 39.1 us -> 0 us
  loops' own time: 23.6 us -> 0 us
    scatter-add x34 -> x0, other arithmetic: 135 us -> none  [the longest x16 60.9 us: edge_sums(): jnp.take(neighbor_proj, flat_index, axis=0) + radial]
    dot_general x164 -> x0, matrix products: 133 us -> none  [the longest x32 34.4 us: edge_sums(): jnp.dot(refined.astype(jnp.bfloat16), w_out, preferred_element_type=jnp.f...]
    reduce_sum x225 -> x0, other arithmetic: 107 us -> none  [the longest x16 20.8 us: edge_sums(): jnp.repeat(center_proj, slot_count, axis=0)]
    gather x50 -> x0, local copies, waits for them, and re-layouts: 93 us -> none  [the longest x32 50.9 us: edge_sums(): jnp.take(all_coords, flat_index, axis=1).reshape(3, block_size, slot_count)]
    pallas_call x0 -> x5, Pallas kernels: none -> 92.5 us  [the longest x2 53.1 us: exchange(): pl.pallas_call(functools.partial(exchange_kernel, sizes, sign), out_shape...]
    reshape x53 -> x0, local copies, waits for them, and re-layouts: 76.9 us -> none  [the longest x16 30.3 us: edge_sums(): jnp.dot(latent_half, w_env, preferred_element_type=jnp.float32)]
    while x1760 -> x0, local copies, waits for them, and re-layouts: 75.9 us -> none
    ppermute x24 -> x0, waiting for transfers between devices: 54.2 us -> none  [from_behind(): lax.ppermute(array, axis, [(i, (i + by) % size) for i in range(size)])]
  transfers between devices with their start and end apart: 24 -> 0, of which waited for: 11 -> 0; matrix products, arithmetic and copies ran while one was open for 2% -> 0% of each run, Pallas kernels for 0% -> 0%
where the time goes in v1:
time: 96.3 us; the launch traced here: 94.8 us
  Pallas kernels  92.5 us (96%)
  local copies, waits for them, and re-layouts  1.65 us (2%)
    pallas_call x2, Pallas kernels, exchange(): pl.pallas_call(functools.partial(exchange_kernel, sizes, sign), out_shape...  53.1 us
    pallas_call x1, Pallas kernels, edges(): pl.pallas_call(edge_kernel, out_shape=(jax.ShapeDtypeStruct((1, ATOMS), f...  33.7 us
    pallas_call x1, Pallas kernels, pack(): pl.pallas_call(pack_kernel, out_shape=(jax.ShapeDtypeStruct((26, MESSAGE,...  3.04 us
    pallas_call x1, Pallas kernels, unpack(): pl.pallas_call(unpack_kernel, out_shape=(jax.ShapeDtypeStruct((3, ATOMS),...  2.62 us

profile of v1, /device:TPU:2, one launch (start us, length us, event | category | flops | bytes accessed | tf_op | source)
XLA Modules:
  0.0 94.8 jit_solution(2807330416991208686)
XLA Ops:
  0.6 1.6 %copy.18.w_env = bf16[256,192]{1,0:T(8,128)(2,1)} copy(bf16[256,192]{0,1:T(8,128)(2,1)} %param.26) | data formatting | bytes 196608 | tf_op args[11]
  2.3 3.0 %pack.1 = (bf16[26,64,256]{2,1,0:T(8,128)(2,1)}, bf16[64,256]{1,0:T(8,128)(2,1)}, bf16[64,256]{1,0:T(8,128)(2,1)}) custom-call(f32[64,256]{1,0:T(8,128)} %features.1, f32[3,64]{1,0:T(4,128)} %positions.3, s32[27,48]{1,0:T(8,128)} %lists.3, bf16[256,256]{1,0:T(8,128)(2,1)} %w_center.3, bf16[256,256]{1,0:T(8,128)(2,1)} %w_neighbor.3), custom_call_target="tpu_custom_call" | custom-call | tf_op jit(solution)/shard_map/pack/pallas_call | solution.py:109
  5.3 28.5 %exchange_out.1.received = bf16[26,64,256]{2,1,0:T(8,128)(2,1)} custom-call(bf16[26,64,256]{2,1,0:T(8,128)(2,1)} %get-tuple-element.13.source), custom_call_target="tpu_custom_call" | custom-call | tf_op jit(solution)/shard_map/exchange_out/pallas_call | solution.py:153
  33.8 33.7 %edges.1 = (f32[1,64]{1,0:T(1,128)}, bf16[26,64,256]{2,1,0:T(8,128)(2,1)}, f32[64,256]{1,0:T(8,128)}, f32[64,256]{1,0:T(8,128)}, f32[8,128]{1,0:T(8,128)}) custom-call(bf16[26,64,256]{2,1,0:T(8,128)(2,1)} %exchange_out.1.received, bf16[64,256]{1,0:T(8,128)(2,1)} %get-tuple-element.14.proj, bf16[64,256]{1,0:T(8,128)(2,1)} %get-tuple-element.15.center, ...), custom_call_target="tpu_custom_call" | custom-call | tf_op jit(solution)/shard_map/edges/pallas_call | solution.py:571
  67.5 24.6 %exchange_back.1.returned = bf16[26,64,256]{2,1,0:T(8,128)(2,1)} custom-call(bf16[26,64,256]{2,1,0:T(8,128)(2,1)} %get-tuple-element.17.source), custom_call_target="tpu_custom_call" | custom-call | tf_op jit(solution)/shard_map/exchange_back/pallas_call | solution.py:153
  92.1 2.6 %unpack.1 = (f32[3,64]{1,0:T(4,128)}, f32[64,256]{1,0:T(8,128)}) custom-call(bf16[26,64,256]{2,1,0:T(8,128)(2,1)} %exchange_back.1.returned, f32[64,256]{1,0:T(8,128)} %get-tuple-element.18.own_proj_grad, f32[64,256]{1,0:T(8,128)} %get-tuple-element.19.center_grad, f32[8,128]{1,0:T(8,128)} %get-tuple-element.20.own_pos_grad, s32[27,48]{1,0:T(8,128)} %lists.3, ...), custom_call_target="tpu_custom_call" | custom-call | tf_op jit(solution)/shard_map/unpack/pallas_call | solution.py:627

commit v2 on v1

--- a/solution.py
+++ b/solution.py
@@ -25,23 +25,32 @@
 BASIS_AT = 1000
 CENTER_AT = 1008
 GROUP = 8
-MESSAGE = 64
 
 f32 = jnp.float32
 bf16 = jnp.bfloat16
 i32 = jnp.int32
 
-DIRECTIONS = [
-    (tx, ty, tz)
-    for tx in (-1, 0, 1)
-    for ty in (-1, 0, 1)
-    for tz in (-1, 0, 1)
-    if (tx, ty, tz) != (0, 0, 0)
+FACES = [(-1, 0, 0), (1, 0, 0), (0, -1, 0), (0, 1, 0), (0, 0, -1), (0, 0, 1)]
+X_FACE, Y_FACE, Z_FACE = 0, 2, 4
+Y_CELLS = [(0, -1, 0), (0, 1, 0)]
+Z_CELLS = [(0, ty, tz) for tz in (-1, 1) for ty in (0, -1, 1)]
+X_CELLS = [
+    (tx,) + behind for tx in (-1, 1) for behind in [(0, 0)] + [c[1:] for c in Y_CELLS + Z_CELLS]
 ]
+DIRECTIONS = Y_CELLS + Z_CELLS + X_CELLS
+Z_AT, X_AT = (2, 5), (8, 17)
 CELLS = [9 * (tx + 1) + 3 * (ty + 1) + tz + 1 for tx, ty, tz in DIRECTIONS]
 SIZES = [math.prod(REACH if t else SIDE for t in d) for d in DIRECTIONS]
 STARTS = [ATOMS + sum(SIZES[:i]) for i in range(26)]
 assert STARTS[-1] + SIZES[-1] == BASIS_AT
+FACE_CELLS = [9 * (tx + 1) + 3 * (ty + 1) + tz + 1 for tx, ty, tz in FACES]
+LIST_ROW = 3
+FACE_LIST = 4
+
+
+def list_slot(direction):
+    tx, ty, tz = direction
+    return 3 * (tx + 1) + (tz + 1 if ty else 1)
 
 
 def nn(a, b):
@@ -84,83 +93,236 @@
     return 0.5 * jnp.tanh(0.5 * x) + 0.5
 
 
-def pack_kernel(features, positions, lists, w_center, w_neighbor, message, proj, center, square, held):
+def pack_kernel(
+    features, positions, lists, w_center, w_neighbor, face_rows, face_small, proj, center, square, listed, held
+):
     rounded = features[...].astype(bf16)
     own = nn(rounded, w_neighbor[...]).astype(bf16)
     proj[...] = own
     center[...] = nn(rounded, w_center[...]).astype(bf16)
     square[...] = jnp.zeros((128, 128), f32)
     square[0:3, 0:ATOMS] = positions[...]
-    high, middle, low = pieces(square[0:8, :])
-    parts = jnp.concatenate([high, middle, low, jnp.zeros((8, 128), f32)], axis=0).astype(bf16)
+    parts = jnp.concatenate(list(pieces(square[0:8, :])), axis=0)
+    parts = jnp.concatenate([parts, jnp.zeros((8, 128), f32)], axis=0).astype(bf16)
     held[0:ATOMS, :] = own
     held[ATOMS:128, :] = jnp.zeros((128 - ATOMS, WIDTH), bf16)
-    square[0:27, 0:GHOST] = lists[...].astype(f32)
+    listed[...] = jnp.full((32, 128), -1.0, f32)
+    listed[0:27, 0:GHOST] = lists[...].astype(f32)
+    square[0:32, :] = listed[...]
     by_entry = square[...].T
     wide = lanes_of((128, 128)).astype(f32)
-    for i, cell in enumerate(CELLS):
+    which = rows_of((8, 128))
+    for i, (face, cell) in enumerate(zip(FACES, FACE_CELLS)):
         chosen = jnp.where(by_entry[:, cell : cell + 1] == wide, 1.0, 0.0).astype(bf16)
-        message[i, 0:GHOST, :] = nn(chosen[0:GHOST], held[...]).astype(bf16)
+        face_rows[i] = nn(chosen[0:GHOST], held[...]).astype(bf16)
         moved = nt(parts, chosen)
-        message[i, GHOST:MESSAGE, :] = jnp.concatenate([moved[0:16], moved[16:32]], axis=1).astype(bf16)
+        small = moved[0:8] + moved[8:16] + moved[16:24]
+        axis = [a for a in range(3) if face[a]][0]
+        for d, c in zip(DIRECTIONS, CELLS):
+            first = 1 if d[1] else 2 if d[2] else 0
+            if first != axis or d[first] != face[first] or first == 0:
+                continue
+            r, half = divmod(list_slot(d), 2)
+            entries = jnp.broadcast_to(listed[c : c + 1, :], (8, 128))
+            if half:
+                entries = pltpu.roll(entries, 64, 1)
+            lane = lanes_of((8, 128))
+            here = (which == LIST_ROW + r) & ((lane >= 64) if half else (lane < 64))
+            small = jnp.where(here, entries, small)
+        face_small[i] = small
 
 
 def pack(features, positions, lists, w_center, w_neighbor):
     return pl.pallas_call(
         pack_kernel,
         out_shape=(
-            jax.ShapeDtypeStruct((26, MESSAGE, WIDTH), bf16),
+            jax.ShapeDtypeStruct((6, GHOST, WIDTH), bf16),
+            jax.ShapeDtypeStruct((6, 8, 128), f32),
             jax.ShapeDtypeStruct((ATOMS, WIDTH), bf16),
             jax.ShapeDtypeStruct((ATOMS, WIDTH), bf16),
         ),
         in_specs=[pl.BlockSpec(memory_space=pltpu.VMEM)] * 5,
-        out_specs=(pl.BlockSpec(memory_space=pltpu.VMEM),) * 3,
-        scratch_shapes=[pltpu.VMEM((128, 128), f32), pltpu.VMEM((128, WIDTH), bf16)],
+        out_specs=(pl.BlockSpec(memory_space=pltpu.VMEM),) * 4,
+        scratch_shapes=[
+            pltpu.VMEM((128, 128), f32),
+            pltpu.VMEM((32, 128), f32),
+            pltpu.VMEM((128, WIDTH), bf16),
+        ],
         name="pack",
     )(features, positions, lists, w_center, w_neighbor)
 
 
-def exchange_kernel(sizes, sign, source, target, send_sem, recv_sem):
+STAGES = 14
+
+
+def neighbours(sizes):
     axes = ("gx", "gy", "gz")
     here = [lax.axis_index(a) for a in axes]
 
-    def place(direction):
+    def place(axis, step):
         return tuple(
-            lax.rem(h + (sign * t + n), n) for h, t, n in zip(here, direction, sizes)
+            lax.rem(h + (step + n), n) if a == axis else h
+            for a, (h, n) in enumerate(zip(here, sizes))
         )
 
     barrier = pltpu.get_barrier_semaphore()
-    for d in DIRECTIONS:
-        pl.semaphore_signal(barrier, inc=1, device_id=place(d), device_id_type=pl.DeviceIdType.MESH)
-    pl.semaphore_wait(barrier, 26)
-    copies = []
-    for i, d in enumerate(DIRECTIONS):
-        copy = pltpu.make_async_remote_copy(
-            src_ref=source.at[i],
-            dst_ref=target.at[i],
-            send_sem=send_sem.at[i],
-            recv_sem=recv_sem.at[i],
-            device_id=place(d),
-            device_id_type=pl.DeviceIdType.MESH,
+    for axis in range(3):
+        for step in (-1, 1):
+            pl.semaphore_signal(
+                barrier, inc=1, device_id=place(axis, step), device_id_type=pl.DeviceIdType.MESH
+            )
+    pl.semaphore_wait(barrier, 6)
+    return place
+
+
+def sender(place, send_sem, recv_sem):
+    count = [0]
+
+    def send(pairs, axis, step):
+        started = []
+        for source, target in pairs:
+            k = count[0]
+            count[0] += 1
+            copy = pltpu.make_async_remote_copy(
+                src_ref=source,
+                dst_ref=target,
+                send_sem=send_sem.at[k],
+                recv_sem=recv_sem.at[k],
+                device_id=place(axis, step),
+                device_id_type=pl.DeviceIdType.MESH,
+            )
+            copy.start()
+            started.append(copy)
+        return started
+
+    return send
+
+
+def arrived(*groups):
+    for group in groups:
+        for copy in group:
+            copy.wait_recv()
+
+
+def sent(*groups):
+    for group in groups:
+        for copy in group:
+            copy.wait_send()
+
+
+def out_kernel(sizes, face_rows, face_small, rows, small, send_sem, recv_sem):
+    send = sender(neighbours(sizes), send_sem, recv_sem)
+    own = [(face_rows, face_small), (rows, small)]
+
+    def move(source, target, count, from_face, axis, step):
+        origin = own[0] if from_face else own[1]
+        return send(
+            [(o.at[pl.ds(source, count)], g.at[pl.ds(target, count)]) for o, g in zip(origin, own[1])],
+            axis,
+            step,
         )
-        copy.start()
-        copies.append(copy)
-    for copy in copies:
-        copy.wait()
-
-
-def exchange(message, sizes, sign):
+
+    steps = ((0, -1), (1, 1))
+    y = [move(Y_FACE + k, k, 1, True, 1, t) for k, t in steps]
+    z_own = [move(Z_FACE + k, Z_AT[k], 1, True, 2, t) for k, t in steps]
+    x_own = [move(X_FACE + k, X_AT[k], 1, True, 0, t) for k, t in steps]
+    arrived(*y)
+    z_pair = [move(0, Z_AT[k] + 1, 2, False, 2, t) for k, t in steps]
+    x_pair = [move(0, X_AT[k] + 1, 2, False, 0, t) for k, t in steps]
+    x_rest = []
+    for half in (0, 1):
+        arrived(z_own[half], z_pair[half])
+        x_rest += [
+            move(Z_AT[half], X_AT[k] + Z_AT[half] + 1, 3, False, 0, t) for k, t in steps
+        ]
+    arrived(*x_own, *x_pair, *x_rest)
+    sent(*y, *z_own, *x_own, *z_pair, *x_pair, *x_rest)
+
+
+def back_kernel(
+    sizes, rows, small, face_rows, face_small, from_x, from_x_small, from_z, from_z_small, total, total_small,
+    send_sem, recv_sem
+):
+    send = sender(neighbours(sizes), send_sem, recv_sem)
+
+    def move(source, target, axis, step):
+        return send(list(zip(source, target)), axis, step)
+
+    def at(refs, start, count):
+        return [r.at[pl.ds(start, count)] for r in refs]
+
+    given, faces = (rows, small), (face_rows, face_small)
+    sums = (total, total_small)
+    steps = ((0, -1), (1, 1))
+    in_x = [(from_x.at[k], from_x_small.at[k]) for k in (0, 1)]
+    in_z = [(from_z.at[k], from_z_small.at[k]) for k in (0, 1)]
+    x_rest = [move(at(given, X_AT[k] + 3, 6), at(in_x[k], 2, 6), 0, -t) for k, t in steps]
+    x_pair = [move(at(given, X_AT[k] + 1, 2), at(in_x[k], 0, 2), 0, -t) for k, t in steps]
+    x_own = [move(at(given, X_AT[k], 1), at(faces, X_FACE + k, 1), 0, -t) for k, t in steps]
+    arrived(*x_rest)
+    for i in range(2, 8):
+        total[i] = (
+            rows[i].astype(f32) + from_x[0, i].astype(f32) + from_x[1, i].astype(f32)
+        ).astype(bf16)
+        total_small[i] = small[i] + from_x_small[0, i] + from_x_small[1, i]
+    z_pair = [move(at(sums, Z_AT[k] + 1, 2), at(in_z[k], 0, 2), 2, -t) for k, t in steps]
+    z_own = [move(at(sums, Z_AT[k], 1), at(faces, Z_FACE + k, 1), 2, -t) for k, t in steps]
+    arrived(*x_pair, *z_pair)
+    for i in range(2):
+        total[i] = (
+            rows[i].astype(f32)
+            + from_x[0, i].astype(f32)
+            + from_x[1, i].astype(f32)
+            + from_z[0, i].astype(f32)
+            + from_z[1, i].astype(f32)
+        ).astype(bf16)
+        total_small[i] = (
+            small[i] + from_x_small[0, i] + from_x_small[1, i] + from_z_small[0, i] + from_z_small[1, i]
+        )
+    y = [move(at(sums, k, 1), at(faces, Y_FACE + k, 1), 1, -t) for k, t in steps]
+    arrived(*x_own, *z_own, *y)
+    sent(*x_rest, *x_pair, *x_own, *z_pair, *z_own, *y)
+
+
+def exchange_out(face_rows, face_small, sizes):
+    vmem = pl.BlockSpec(memory_space=pltpu.VMEM)
     return pl.pallas_call(
-        functools.partial(exchange_kernel, sizes, sign),
-        out_shape=jax.ShapeDtypeStruct(message.shape, message.dtype),
-        in_specs=[pl.BlockSpec(memory_space=pl.ANY)],
-        out_specs=pl.BlockSpec(memory_space=pl.ANY),
-        scratch_shapes=[pltpu.SemaphoreType.DMA((26,)), pltpu.SemaphoreType.DMA((26,))],
-        compiler_params=pltpu.CompilerParams(
-            collective_id=0 if sign > 0 else 1, has_side_effects=True
+        functools.partial(out_kernel, sizes),
+        out_shape=(
+            jax.ShapeDtypeStruct((26, GHOST, WIDTH), bf16),
+            jax.ShapeDtypeStruct((26, 8, 128), f32),
         ),
-        name="exchange_out" if sign > 0 else "exchange_back",
-    )(message)
+        in_specs=[vmem] * 2,
+        out_specs=(vmem,) * 2,
+        scratch_shapes=[pltpu.SemaphoreType.DMA((2 * STAGES,)), pltpu.SemaphoreType.DMA((2 * STAGES,))],
+        compiler_params=pltpu.CompilerParams(collective_id=0, has_side_effects=True),
+        name="exchange_out",
+    )(face_rows, face_small)
+
+
+def exchange_back(rows, small, sizes):
+    vmem = pl.BlockSpec(memory_space=pltpu.VMEM)
+    return pl.pallas_call(
+        functools.partial(back_kernel, sizes),
+        out_shape=(
+            jax.ShapeDtypeStruct((6, GHOST, WIDTH), bf16),
+            jax.ShapeDtypeStruct((6, 8, 128), f32),
+        ),
+        in_specs=[vmem] * 2,
+        out_specs=(vmem,) * 2,
+        scratch_shapes=[
+            pltpu.VMEM((2, 8, GHOST, WIDTH), bf16),
+            pltpu.VMEM((2, 8, 8, 128), f32),
+            pltpu.VMEM((2, 2, GHOST, WIDTH), bf16),
+            pltpu.VMEM((2, 2, 8, 128), f32),
+            pltpu.VMEM((8, GHOST, WIDTH), bf16),
+            pltpu.VMEM((8, 8, 128), f32),
+            pltpu.SemaphoreType.DMA((2 * 12,)),
+            pltpu.SemaphoreType.DMA((2 * 12,)),
+        ],
+        compiler_params=pltpu.CompilerParams(collective_id=1, has_side_effects=True),
+        name="exchange_back",
+    )(rows, small)
 
 
 R_INDEX, R_ENV, R_SCALED, R_SCALE, R_SLOPE, R_U, R_INV, R_Y, R_BESS, R_BESS_D = 0, 1, 2, 3, 4, 5, 8, 9, 17, 25
@@ -368,6 +530,7 @@
 
 def edge_kernel(
     received,
+    received_small,
     proj,
     center,
     positions,
@@ -383,11 +546,14 @@
     w_final,
     energy_out,
     back,
+    back_small,
     own_proj_grad,
     center_grad,
     own_pos_grad,
     rows,
     tail_rows,
+    lists,
+    faces,
     coords,
     head_proj,
     tail_proj,
@@ -403,8 +569,27 @@
     energy,
 ):
     rows[0:ATOMS, :] = proj[...].astype(f32)
+    lane = lanes_of((8, 128))
+    lists[...] = jnp.full((128, 128), -1.0, f32)
+    faces[...] = jnp.full((128, 128), -2.0, f32)
+    corner = [i for i in range(26) if DIRECTIONS[i] not in FACES]
+    for i in corner:
+        r, half = divmod(list_slot(DIRECTIONS[i]), 2)
+        entries = received_small[i, LIST_ROW + r : LIST_ROW + r + 1, :]
+        lists[i : i + 1, :] = pltpu.roll(entries, 64, 1) if half else entries
+        r = LIST_ROW + FACE_LIST // 2
+        faces[i : i + 1, :] = jnp.where(lane[0:1] < GHOST, received_small[i, r : r + 1, :], -2.0)
+    entry_col = lists[...].T
+    face_col = faces[...].T
+    chosen = {
+        i: jnp.where(entry_col[:, i : i + 1] == faces[i : i + 1, :], 1.0, 0.0).astype(bf16) for i in corner
+    }
     for i in range(26):
-        rows[STARTS[i] : STARTS[i] + SIZES[i], :] = received[i, 0:GHOST, :].astype(f32)[0 : SIZES[i]]
+        if i in chosen:
+            value = nn(chosen[i][0:GHOST, 0:GHOST], received[i])
+        else:
+            value = received[i].astype(f32)
+        rows[STARTS[i] : STARTS[i] + SIZES[i], :] = value[0 : SIZES[i]]
     rows[BASIS_AT:CENTER_AT, :] = w_basis[...].astype(f32)
     rows[CENTER_AT:LIST, :] = jnp.zeros((LIST - CENTER_AT, WIDTH), f32)
     for k in range(HEAD // 128):
@@ -413,14 +598,16 @@
         rows[CENTER_AT : CENTER_AT + GROUP, :] = center[...].astype(f32)[GROUP * b : GROUP * b + GROUP]
         tail_proj[b] = rows[HEAD:LIST, :].T.astype(bf16)
 
-    lane = lanes_of((8, 128))
     coords[...] = jnp.zeros(coords.shape, f32)
     coords[0:3, 0:ATOMS] = positions[...]
     filled = [coords[0:8, 128 * k : 128 * k + 128] for k in range(8)]
     which = rows_of((8, 128))
     for i, d in enumerate(DIRECTIONS):
-        block = received[i, GHOST:MESSAGE, :].astype(f32)
-        value = block[0:8, 0:128] + block[8:16, 0:128] + block[0:8, 128:256]
+        value = received_small[i]
+        if i in chosen:
+            parts = jnp.concatenate(list(pieces(value)) + [jnp.zeros((8, 128), f32)], axis=0)
+            parts = nt(parts.astype(bf16), chosen[i])
+            value = parts[0:8] + parts[8:16] + parts[16:24]
         step = [t * SIDE * SPACING for t in d]
         shift = jnp.where(which == 0, step[0], jnp.where(which == 1, step[1], step[2]))
         value = value - shift
@@ -547,7 +734,13 @@
             value = tail_rows[0:GHOST, :]
         elif SIZES[i] < GHOST:
             value = jnp.where(entry < SIZES[i], value, 0.0)
-        back[i, 0:GHOST, :] = value.astype(bf16)
+        value = value.astype(bf16)
+        if i in chosen:
+            back_chosen = jnp.where(
+                face_col[:, i : i + 1] == jnp.where(lane[0:1] < SIZES[i], lists[i : i + 1, :], -1.0), 1.0, 0.0
+            ).astype(bf16)
+            value = nn(back_chosen[0:GHOST, 0:GHOST], value).astype(bf16)
+        back[i] = value
         k, at = divmod(STARTS[i], 128)
         moved = coord_grad[k]
         if at:
@@ -555,33 +748,33 @@
         if at + SIZES[i] > 128:
             moved = jnp.where(lane < 128 - at, moved, pltpu.roll(coord_grad[k + 1], 128 - at, 1))
         moved = jnp.where(lane < SIZES[i], moved, 0.0)
-        high, middle, lowest = pieces(moved)
-        back[i, GHOST:MESSAGE, :] = jnp.concatenate(
-            [
-                jnp.concatenate([high, middle], axis=0),
-                jnp.concatenate([lowest, jnp.zeros((8, 128), f32)], axis=0),
-            ],
-            axis=1,
-        ).astype(bf16)
-
-
-def edges(received, proj, center, positions, species, neighbor, live, scale, shift, *weights):
+        if i in chosen:
+            parts = jnp.concatenate(list(pieces(moved)) + [jnp.zeros((8, 128), f32)], axis=0)
+            parts = nt(parts.astype(bf16), back_chosen)
+            moved = parts[0:8] + parts[8:16] + parts[16:24]
+        back_small[i] = moved
+
+
+def edges(received, received_small, proj, center, positions, species, neighbor, live, scale, shift, *weights):
     vmem = pl.BlockSpec(memory_space=pltpu.VMEM)
     smem = pl.BlockSpec(memory_space=pltpu.SMEM)
     return pl.pallas_call(
         edge_kernel,
         out_shape=(
             jax.ShapeDtypeStruct((1, ATOMS), f32),
-            jax.ShapeDtypeStruct((26, MESSAGE, WIDTH), bf16),
+            jax.ShapeDtypeStruct((26, GHOST, WIDTH), bf16),
+            jax.ShapeDtypeStruct((26, 8, 128), f32),
             jax.ShapeDtypeStruct((ATOMS, WIDTH), f32),
             jax.ShapeDtypeStruct((ATOMS, WIDTH), f32),
             jax.ShapeDtypeStruct((8, 128), f32),
         ),
-        in_specs=[vmem] * 7 + [smem] * 2 + [vmem] * 5,
-        out_specs=(vmem,) * 5,
+        in_specs=[vmem] * 8 + [smem] * 2 + [vmem] * 5,
+        out_specs=(vmem,) * 6,
         scratch_shapes=[
             pltpu.VMEM((LIST, WIDTH), f32),
             pltpu.VMEM((128, WIDTH), f32),
+            pltpu.VMEM((128, 128), f32),
+            pltpu.VMEM((128, 128), f32),
             pltpu.VMEM((8, LIST), f32),
             pltpu.VMEM((WIDTH, HEAD), bf16),
             pltpu.VMEM((8, WIDTH, 128), bf16),
@@ -598,23 +791,25 @@
         ],
         compiler_params=pltpu.CompilerParams(vmem_limit_bytes=56 * 1024 * 1024),
         name="edges",
-    )(received, proj, center, positions, species, neighbor, live, scale, shift, *weights)
+    )(
+        received, received_small, proj, center, positions, species, neighbor, live, scale, shift, *weights
+    )
 
 
 def unpack_kernel(
-    returned, own_proj_grad, center_grad, own_pos_grad, lists, w_center, w_neighbor, forces, feature_grad, padded
+    face_rows, face_small, own_proj_grad, center_grad, own_pos_grad, lists, w_center, w_neighbor, forces,
+    feature_grad, padded
 ):
     padded[...] = jnp.full((32, 128), -1, i32)
     padded[0:27, 0:GHOST] = lists[...]
     proj_grad = own_proj_grad[...]
     pos_grad = jnp.zeros((32, ATOMS), f32)
-    atom = rows_of((ATOMS, GHOST))
-    for i, cell in enumerate(CELLS):
-        chosen = jnp.where(padded[cell : cell + 1, 0:GHOST] == atom, 1.0, 0.0).astype(bf16)
-        proj_grad = proj_grad + nn(chosen, returned[i, 0:GHOST, :])
-        block = returned[i, GHOST:MESSAGE, :]
-        parts = jnp.concatenate([block[:, 0:GHOST], block[:, 128 : 128 + GHOST]], axis=0)
-        pos_grad = pos_grad + nt(parts, chosen)
+    atom = rows_of((ATOMS, 128))
+    for i, cell in enumerate(FACE_CELLS):
+        chosen = jnp.where(padded[cell : cell + 1, :] == atom, 1.0, 0.0).astype(bf16)
+        proj_grad = proj_grad + nn(chosen[:, 0:GHOST], face_rows[i])
+        parts = jnp.concatenate(list(pieces(face_small[i])) + [jnp.zeros((8, 128), f32)], axis=0)
+        pos_grad = pos_grad + nt(parts.astype(bf16), chosen)
     feature_grad[...] = nt(proj_grad.astype(bf16), w_neighbor[...]) + nt(
         center_grad[...].astype(bf16), w_center[...]
     )
@@ -630,7 +825,7 @@
             jax.ShapeDtypeStruct((3, ATOMS), f32),
             jax.ShapeDtypeStruct((ATOMS, WIDTH), f32),
         ),
-        in_specs=[vmem] * 7,
+        in_specs=[vmem] * 8,
         out_specs=(vmem,) * 2,
         scratch_shapes=[pltpu.VMEM((32, 128), i32)],
         name="unpack",
@@ -657,10 +852,13 @@
         w_out,
         w_final,
     ):
-        message, proj, center = pack(atom_features, positions, send_list, w_center, w_neighbor)
-        received = exchange(message, sizes, 1)
-        energy, back, own_proj_grad, center_grad, own_pos_grad = edges(
+        face_rows, face_small, proj, center = pack(
+            atom_features, positions, send_list, w_center, w_neighbor
+        )
+        received, received_small = exchange_out(face_rows, face_small, sizes)
+        energy, back, back_small, own_proj_grad, center_grad, own_pos_grad = edges(
             received,
+            received_small,
             proj,
             center,
             positions,
@@ -675,9 +873,9 @@
             w_out,
             w_final.reshape(1, OUT_WIDTH),
         )
-        returned = exchange(back, sizes, -1)
+        face_rows, face_small = exchange_back(back, back_small, sizes)
         forces, feature_grad = unpack(
-            returned, own_proj_grad, center_grad, own_pos_grad, send_list, w_center, w_neighbor
+            face_rows, face_small, own_proj_grad, center_grad, own_pos_grad, send_list, w_center, w_neighbor
         )
         return energy.reshape(ATOMS), forces, feature_grad
 

time: 96.3 us -> 80.7 us (0.84); the launches traced: 94.8 us -> 80.4 us
  Pallas kernels: 92.5 us -> 78 us
    pallas_call x3, Pallas kernels: 56.1 us -> 41.3 us  [the longest x1 20.4 us: exchange_out(): pl.pallas_call(functools.partial(out_kernel, sizes), out_shape=(jax.Shape...]
where the time goes in v2:
time: 80.7 us; the launch traced here: 80.4 us
  Pallas kernels  78 us (97%)
  local copies, waits for them, and re-layouts  1.66 us (2%)
    pallas_call x1, Pallas kernels, edges(): pl.pallas_call(edge_kernel, out_shape=(jax.ShapeDtypeStruct((1, ATOMS), f...  34.6 us
    pallas_call x1, Pallas kernels, exchange_out(): pl.pallas_call(functools.partial(out_kernel, sizes), out_shape=(jax.Shape...  20.4 us
    pallas_call x1, Pallas kernels, exchange_back(): pl.pallas_call(functools.partial(back_kernel, sizes), out_shape=(jax.Shap...  18.7 us
    pallas_call x1, Pallas kernels, pack(): pl.pallas_call(pack_kernel, out_shape=(jax.ShapeDtypeStruct((6, GHOST, WI...  2.15 us
    pallas_call x1, Pallas kernels, unpack(): pl.pallas_call(unpack_kernel, out_shape=(jax.ShapeDtypeStruct((3, ATOMS),...  2.13 us
    unnamed x1, local copies, waits for them, and re-layouts  1.66 us

profile of v2, /device:TPU:2, one launch (start us, length us, event | category | flops | bytes accessed | tf_op | source)
XLA Modules:
  0.0 80.4 jit_solution(14006088769627318691)
XLA Ops:
  0.6 1.7 %copy.18.w_env = bf16[256,192]{1,0:T(8,128)(2,1)} copy(bf16[256,192]{0,1:T(8,128)(2,1)} %param.26) | data formatting | bytes 196608 | tf_op args[11]
  2.3 2.1 %pack.1 = (bf16[6,48,256]{2,1,0:T(8,128)(2,1)}, f32[6,8,128]{2,1,0:T(8,128)}, bf16[64,256]{1,0:T(8,128)(2,1)}, bf16[64,256]{1,0:T(8,128)(2,1)}) custom-call(f32[64,256]{1,0:T(8,128)} %features.1, f32[3,64]{1,0:T(4,128)} %positions.3, s32[27,48]{1,0:T(8,128)} %lists.3, bf16[256,256]{1,0:T(8,128)(2,1)} %w_center.3, bf16[256,256]{1,0:T(8,128)(2,1)} %w_neighbor.3), custom_call_target="tpu_custom_call" | custom-call | tf_op jit(solution)/shard_map/pack/pallas_call | solution.py:136
  4.4 20.4 %exchange_out.1 = (bf16[26,48,256]{2,1,0:T(8,128)(2,1)}, f32[26,8,128]{2,1,0:T(8,128)}) custom-call(bf16[6,48,256]{2,1,0:T(8,128)(2,1)} %get-tuple-element.19.face_rows, f32[6,8,128]{2,1,0:T(8,128)} %get-tuple-element.20.face_small), custom_call_target="tpu_custom_call" | custom-call | tf_op jit(solution)/shard_map/exchange_out/pallas_call | solution.py:289
  24.9 34.6 %edges.1 = (f32[1,64]{1,0:T(1,128)}, bf16[26,48,256]{2,1,0:T(8,128)(2,1)}, f32[26,8,128]{2,1,0:T(8,128)}, f32[64,256]{1,0:T(8,128)}, f32[64,256]{1,0:T(8,128)}, /*index=5*/f32[8,128]{1,0:T(8,128)}) custom-call(bf16[26,48,256]{2,1,0:T(8,128)(2,1)} %get-tuple-element.21.received, f32[26,8,128]{2,1,0:T(8,128)} %get-tuple-element.22.received_small, ...), custom_call_target="tpu_custom_call" | custom-call | tf_op jit(solution)/shard_map/edges/pallas_call | solution.py:761
  59.6 18.7 %exchange_back.1 = (bf16[6,48,256]{2,1,0:T(8,128)(2,1)}, f32[6,8,128]{2,1,0:T(8,128)}) custom-call(bf16[26,48,256]{2,1,0:T(8,128)(2,1)} %get-tuple-element.26.rows, f32[26,8,128]{2,1,0:T(8,128)} %get-tuple-element.27.small), custom_call_target="tpu_custom_call" | custom-call | tf_op jit(solution)/shard_map/exchange_back/pallas_call | solution.py:305
  78.2 2.1 %unpack.1 = (f32[3,64]{1,0:T(4,128)}, f32[64,256]{1,0:T(8,128)}) custom-call(bf16[6,48,256]{2,1,0:T(8,128)(2,1)} %get-tuple-element.28.face_rows, f32[6,8,128]{2,1,0:T(8,128)} %get-tuple-element.29.face_small, f32[64,256]{1,0:T(8,128)} %get-tuple-element.30.own_proj_grad, f32[64,256]{1,0:T(8,128)} %get-tuple-element.31.center_grad, ...), custom_call_target="tpu_custom_call" | custom-call | tf_op jit(solution)/shard_map/unpack/pallas_call | solution.py:822

commit v3 on v2

--- a/solution.py
+++ b/solution.py
@@ -25,6 +25,7 @@
 BASIS_AT = 1000
 CENTER_AT = 1008
 GROUP = 8
+ABREAST = 4
 
 f32 = jnp.float32
 bf16 = jnp.bfloat16
@@ -93,9 +94,70 @@
     return 0.5 * jnp.tanh(0.5 * x) + 0.5
 
 
-def pack_kernel(
-    features, positions, lists, w_center, w_neighbor, face_rows, face_small, proj, center, square, listed, held
+PARTNERS = Y_CELLS + Z_CELLS + FACES[0:2]
+
+
+def greet(sizes):
+    here = [lax.axis_index(a) for a in ("gx", "gy", "gz")]
+
+    def place(direction):
+        return tuple(lax.rem(h + (t + n), n) if t else h for h, t, n in zip(here, direction, sizes))
+
+    barrier = pltpu.get_barrier_semaphore()
+    for d in PARTNERS:
+        pl.semaphore_signal(barrier, inc=1, device_id=place(d), device_id_type=pl.DeviceIdType.MESH)
+    return place, barrier
+
+
+def sender(place, send_sem, recv_sem):
+    count = [0]
+
+    def send(sources, targets, direction):
+        started = []
+        for source, target in zip(sources, targets):
+            k = count[0]
+            count[0] += 1
+            copy = pltpu.make_async_remote_copy(
+                src_ref=source,
+                dst_ref=target,
+                send_sem=send_sem.at[k],
+                recv_sem=recv_sem.at[k],
+                device_id=place(direction),
+                device_id_type=pl.DeviceIdType.MESH,
+            )
+            copy.start()
+            started.append(copy)
+        return started
+
+    return send
+
+
+def arrived(*groups):
+    for group in groups:
+        for copy in group:
+            copy.wait_recv()
+
+
+def sent(*groups):
+    for group in groups:
+        for copy in group:
+            copy.wait_send()
+
+
+def at(refs, start, count):
+    return [r.at[pl.ds(start, count)] for r in refs]
+
+
+def first_face(direction):
+    tx, ty, tz = direction
+    return Y_FACE + (ty + 1) // 2 if ty else Z_FACE + (tz + 1) // 2 if tz else X_FACE + (tx + 1) // 2
+
+
+def out_kernel(
+    sizes, features, positions, lists, w_center, w_neighbor, rows, small, proj, center, square, listed, held,
+    face_rows, face_small, send_sem, recv_sem
 ):
+    place, barrier = greet(sizes)
     rounded = features[...].astype(bf16)
     own = nn(rounded, w_neighbor[...]).astype(bf16)
     proj[...] = own
@@ -116,7 +178,7 @@
         chosen = jnp.where(by_entry[:, cell : cell + 1] == wide, 1.0, 0.0).astype(bf16)
         face_rows[i] = nn(chosen[0:GHOST], held[...]).astype(bf16)
         moved = nt(parts, chosen)
-        small = moved[0:8] + moved[8:16] + moved[16:24]
+        packed = moved[0:8] + moved[8:16] + moved[16:24]
         axis = [a for a in range(3) if face[a]][0]
         for d, c in zip(DIRECTIONS, CELLS):
             first = 1 if d[1] else 2 if d[2] else 0
@@ -128,200 +190,99 @@
                 entries = pltpu.roll(entries, 64, 1)
             lane = lanes_of((8, 128))
             here = (which == LIST_ROW + r) & ((lane >= 64) if half else (lane < 64))
-            small = jnp.where(here, entries, small)
-        face_small[i] = small
-
-
-def pack(features, positions, lists, w_center, w_neighbor):
-    return pl.pallas_call(
-        pack_kernel,
-        out_shape=(
-            jax.ShapeDtypeStruct((6, GHOST, WIDTH), bf16),
-            jax.ShapeDtypeStruct((6, 8, 128), f32),
-            jax.ShapeDtypeStruct((ATOMS, WIDTH), bf16),
-            jax.ShapeDtypeStruct((ATOMS, WIDTH), bf16),
-        ),
-        in_specs=[pl.BlockSpec(memory_space=pltpu.VMEM)] * 5,
-        out_specs=(pl.BlockSpec(memory_space=pltpu.VMEM),) * 4,
-        scratch_shapes=[
-            pltpu.VMEM((128, 128), f32),
-            pltpu.VMEM((32, 128), f32),
-            pltpu.VMEM((128, WIDTH), bf16),
-        ],
-        name="pack",
-    )(features, positions, lists, w_center, w_neighbor)
-
-
-STAGES = 14
-
-
-def neighbours(sizes):
-    axes = ("gx", "gy", "gz")
-    here = [lax.axis_index(a) for a in axes]
-
-    def place(axis, step):
-        return tuple(
-            lax.rem(h + (step + n), n) if a == axis else h
-            for a, (h, n) in enumerate(zip(here, sizes))
-        )
-
-    barrier = pltpu.get_barrier_semaphore()
-    for axis in range(3):
-        for step in (-1, 1):
-            pl.semaphore_signal(
-                barrier, inc=1, device_id=place(axis, step), device_id_type=pl.DeviceIdType.MESH
-            )
-    pl.semaphore_wait(barrier, 6)
-    return place
-
-
-def sender(place, send_sem, recv_sem):
-    count = [0]
-
-    def send(pairs, axis, step):
-        started = []
-        for source, target in pairs:
-            k = count[0]
-            count[0] += 1
-            copy = pltpu.make_async_remote_copy(
-                src_ref=source,
-                dst_ref=target,
-                send_sem=send_sem.at[k],
-                recv_sem=recv_sem.at[k],
-                device_id=place(axis, step),
-                device_id_type=pl.DeviceIdType.MESH,
-            )
-            copy.start()
-            started.append(copy)
-        return started
-
-    return send
-
-
-def arrived(*groups):
-    for group in groups:
-        for copy in group:
-            copy.wait_recv()
-
-
-def sent(*groups):
-    for group in groups:
-        for copy in group:
-            copy.wait_send()
-
-
-def out_kernel(sizes, face_rows, face_small, rows, small, send_sem, recv_sem):
-    send = sender(neighbours(sizes), send_sem, recv_sem)
-    own = [(face_rows, face_small), (rows, small)]
-
-    def move(source, target, count, from_face, axis, step):
-        origin = own[0] if from_face else own[1]
-        return send(
-            [(o.at[pl.ds(source, count)], g.at[pl.ds(target, count)]) for o, g in zip(origin, own[1])],
-            axis,
-            step,
-        )
-
-    steps = ((0, -1), (1, 1))
-    y = [move(Y_FACE + k, k, 1, True, 1, t) for k, t in steps]
-    z_own = [move(Z_FACE + k, Z_AT[k], 1, True, 2, t) for k, t in steps]
-    x_own = [move(X_FACE + k, X_AT[k], 1, True, 0, t) for k, t in steps]
-    arrived(*y)
-    z_pair = [move(0, Z_AT[k] + 1, 2, False, 2, t) for k, t in steps]
-    x_pair = [move(0, X_AT[k] + 1, 2, False, 0, t) for k, t in steps]
-    x_rest = []
-    for half in (0, 1):
-        arrived(z_own[half], z_pair[half])
-        x_rest += [
-            move(Z_AT[half], X_AT[k] + Z_AT[half] + 1, 3, False, 0, t) for k, t in steps
+            packed = jnp.where(here, entries, packed)
+        face_small[i] = packed
+    pl.semaphore_wait(barrier, len(PARTNERS))
+    send = sender(place, send_sem, recv_sem)
+    own, cells = (face_rows, face_small), (rows, small)
+    direct = {}
+    for i in sorted(range(8), key=lambda i: (i < 2, i)):
+        d = DIRECTIONS[i]
+        direct[i] = send(at(own, first_face(d), 1), at(cells, i, 1), d)
+    steps = ((0, FACES[0]), (1, FACES[1]))
+    x_own = [send(at(own, X_FACE + k, 1), at(cells, X_AT[k], 1), d) for k, d in steps]
+    onward = []
+    for start, count in ((0, 2), (2, 3), (5, 3)):
+        arrived(*[direct[i] for i in range(start, start + count)])
+        onward += [
+            send(at(cells, start, count), at(cells, X_AT[k] + 1 + start, count), d) for k, d in steps
         ]
-    arrived(*x_own, *x_pair, *x_rest)
-    sent(*y, *z_own, *x_own, *z_pair, *x_pair, *x_rest)
-
-
-def back_kernel(
-    sizes, rows, small, face_rows, face_small, from_x, from_x_small, from_z, from_z_small, total, total_small,
-    send_sem, recv_sem
-):
-    send = sender(neighbours(sizes), send_sem, recv_sem)
-
-    def move(source, target, axis, step):
-        return send(list(zip(source, target)), axis, step)
-
-    def at(refs, start, count):
-        return [r.at[pl.ds(start, count)] for r in refs]
-
-    given, faces = (rows, small), (face_rows, face_small)
-    sums = (total, total_small)
-    steps = ((0, -1), (1, 1))
-    in_x = [(from_x.at[k], from_x_small.at[k]) for k in (0, 1)]
-    in_z = [(from_z.at[k], from_z_small.at[k]) for k in (0, 1)]
-    x_rest = [move(at(given, X_AT[k] + 3, 6), at(in_x[k], 2, 6), 0, -t) for k, t in steps]
-    x_pair = [move(at(given, X_AT[k] + 1, 2), at(in_x[k], 0, 2), 0, -t) for k, t in steps]
-    x_own = [move(at(given, X_AT[k], 1), at(faces, X_FACE + k, 1), 0, -t) for k, t in steps]
-    arrived(*x_rest)
-    for i in range(2, 8):
-        total[i] = (
-            rows[i].astype(f32) + from_x[0, i].astype(f32) + from_x[1, i].astype(f32)
-        ).astype(bf16)
-        total_small[i] = small[i] + from_x_small[0, i] + from_x_small[1, i]
-    z_pair = [move(at(sums, Z_AT[k] + 1, 2), at(in_z[k], 0, 2), 2, -t) for k, t in steps]
-    z_own = [move(at(sums, Z_AT[k], 1), at(faces, Z_FACE + k, 1), 2, -t) for k, t in steps]
-    arrived(*x_pair, *z_pair)
-    for i in range(2):
-        total[i] = (
-            rows[i].astype(f32)
-            + from_x[0, i].astype(f32)
-            + from_x[1, i].astype(f32)
-            + from_z[0, i].astype(f32)
-            + from_z[1, i].astype(f32)
-        ).astype(bf16)
-        total_small[i] = (
-            small[i] + from_x_small[0, i] + from_x_small[1, i] + from_z_small[0, i] + from_z_small[1, i]
-        )
-    y = [move(at(sums, k, 1), at(faces, Y_FACE + k, 1), 1, -t) for k, t in steps]
-    arrived(*x_own, *z_own, *y)
-    sent(*x_rest, *x_pair, *x_own, *z_pair, *z_own, *y)
-
-
-def exchange_out(face_rows, face_small, sizes):
+    arrived(*x_own, *onward)
+    sent(*direct.values(), *x_own, *onward)
+
+
+def send_out(features, positions, lists, w_center, w_neighbor, sizes):
     vmem = pl.BlockSpec(memory_space=pltpu.VMEM)
     return pl.pallas_call(
         functools.partial(out_kernel, sizes),
         out_shape=(
             jax.ShapeDtypeStruct((26, GHOST, WIDTH), bf16),
             jax.ShapeDtypeStruct((26, 8, 128), f32),
+            jax.ShapeDtypeStruct((ATOMS, WIDTH), bf16),
+            jax.ShapeDtypeStruct((ATOMS, WIDTH), bf16),
         ),
-        in_specs=[vmem] * 2,
-        out_specs=(vmem,) * 2,
-        scratch_shapes=[pltpu.SemaphoreType.DMA((2 * STAGES,)), pltpu.SemaphoreType.DMA((2 * STAGES,))],
+        in_specs=[vmem] * 5,
+        out_specs=(vmem,) * 4,
+        scratch_shapes=[
+            pltpu.VMEM((128, 128), f32),
+            pltpu.VMEM((32, 128), f32),
+            pltpu.VMEM((128, WIDTH), bf16),
+            pltpu.VMEM((6, GHOST, WIDTH), bf16),
+            pltpu.VMEM((6, 8, 128), f32),
+            pltpu.SemaphoreType.DMA((32,)),
+            pltpu.SemaphoreType.DMA((32,)),
+        ],
         compiler_params=pltpu.CompilerParams(collective_id=0, has_side_effects=True),
-        name="exchange_out",
-    )(face_rows, face_small)
-
-
-def exchange_back(rows, small, sizes):
+        name="send_out",
+    )(features, positions, lists, w_center, w_neighbor)
+
+
+def back_kernel(
+    sizes, rows, small, owner_rows, owner_small, from_x, from_x_small, total, total_small, send_sem, recv_sem
+):
+    place, barrier = greet(sizes)
+    pl.semaphore_wait(barrier, len(PARTNERS))
+    send = sender(place, send_sem, recv_sem)
+    given, sums, owners = (rows, small), (total, total_small), (owner_rows, owner_small)
+    steps = ((0, FACES[1]), (1, FACES[0]))
+    in_x = [(from_x.at[k], from_x_small.at[k]) for k in (0, 1)]
+    x_rest = [send(at(given, X_AT[k] + 3, 6), at(in_x[k], 2, 6), d) for k, d in steps]
+    x_pair = [send(at(given, X_AT[k] + 1, 2), at(in_x[k], 0, 2), d) for k, d in steps]
+    x_own = [send(at(given, X_AT[k], 1), at(owners, 8 + k, 1), d) for k, d in steps]
+    direct = []
+    for group, cells in ((x_rest, range(2, 8)), (x_pair, range(2))):
+        arrived(*group)
+        for i in cells:
+            total[i] = (
+                rows[i].astype(f32) + from_x[0, i].astype(f32) + from_x[1, i].astype(f32)
+            ).astype(bf16)
+            total_small[i] = small[i] + from_x_small[0, i] + from_x_small[1, i]
+            d = tuple(-t for t in DIRECTIONS[i])
+            direct.append(send(at(sums, i, 1), at(owners, i, 1), d))
+    arrived(*x_own, *direct)
+    sent(*x_rest, *x_pair, *x_own, *direct)
+
+
+def send_back(rows, small, sizes):
     vmem = pl.BlockSpec(memory_space=pltpu.VMEM)
     return pl.pallas_call(
         functools.partial(back_kernel, sizes),
         out_shape=(
-            jax.ShapeDtypeStruct((6, GHOST, WIDTH), bf16),
-            jax.ShapeDtypeStruct((6, 8, 128), f32),
+            jax.ShapeDtypeStruct((10, GHOST, WIDTH), bf16),
+            jax.ShapeDtypeStruct((10, 8, 128), f32),
         ),
         in_specs=[vmem] * 2,
         out_specs=(vmem,) * 2,
         scratch_shapes=[
             pltpu.VMEM((2, 8, GHOST, WIDTH), bf16),
             pltpu.VMEM((2, 8, 8, 128), f32),
-            pltpu.VMEM((2, 2, GHOST, WIDTH), bf16),
-            pltpu.VMEM((2, 2, 8, 128), f32),
             pltpu.VMEM((8, GHOST, WIDTH), bf16),
             pltpu.VMEM((8, 8, 128), f32),
-            pltpu.SemaphoreType.DMA((2 * 12,)),
-            pltpu.SemaphoreType.DMA((2 * 12,)),
+            pltpu.SemaphoreType.DMA((28,)),
+            pltpu.SemaphoreType.DMA((28,)),
         ],
         compiler_params=pltpu.CompilerParams(collective_id=1, has_side_effects=True),
-        name="exchange_back",
+        name="send_back",
     )(rows, small)
 
 
@@ -387,6 +348,7 @@
     energy,
 ):
     width = GROUP * per_atom
+    abreast = 1 if per_atom == SLOTS else ABREAST
     lane = lanes_of((GROUP, 128))
 
     def chunks_of(q):
@@ -426,7 +388,7 @@
         | ((deg == 2) & (comp >= 4) & (comp <= 8))
     )
 
-    def block(b, carry):
+    def block(b, onehot):
         def value(q):
             parts = [table[k, pl.ds(q * GROUP + b, 1), :] for k in range(width // 128)]
             return jnp.concatenate(parts, axis=1)
@@ -451,12 +413,14 @@
         ).astype(bf16)
         hot = onehot[:, 0:width]
 
+        yield
         pre = nn(jnp.concatenate([head_proj[...], tail_proj[b]], axis=1), hot)
         sig = sigmoid(pre)
         act = pre * sig
         act_d = sig + act * (1.0 - sig)
         latent = env * act
         latent_h = latent.astype(bf16)
+        yield
         weights = nn(env_t[...], latent_h)
         weights_h = weights.astype(bf16)
         ys = eight(R_Y)
@@ -466,15 +430,19 @@
             + [jnp.zeros(wide, f32)],
             axis=0,
         ).astype(bf16)
+        yield
         around = jnp.where(allowed, ENV_NORM * nt(weights_h, harm), 0.0)
         around_h = around.astype(bf16)
+        yield
         tensor = nn(around_h, harm)
         scalars_h = (weights * tensor).astype(bf16)
+        yield
         mixed = nn(latent_t[...], jnp.concatenate([latent_h, scalars_h], axis=0))
         sig = sigmoid(mixed)
         update = mixed * sig
         update_d = sig + update * (1.0 - sig)
         refined_h = (latent + env * update).astype(bf16)
+        yield
         hidden = nn(out_t[...], refined_h)
         sig = sigmoid(hidden)
         hidden_act = hidden * sig
@@ -486,18 +454,24 @@
 
         scaled = value(R_SCALED)
         d_hidden = ((sig + hidden_act * (1.0 - sig)) * final * scaled).astype(bf16)
+        yield
         d_refined = nn(w_out[...], d_hidden)
         d_env = value(R_SCALE) * per_edge
         d_env += jnp.sum(d_refined * update, axis=0, keepdims=True)
         d_mixed = (env * d_refined * update_d).astype(bf16)
+        yield
         d_both = nn(w_latent[...], d_mixed)
         d_scalars = d_both[WIDTH:]
         d_tensor_h = (d_scalars * weights).astype(bf16)
+        yield
         d_around = jnp.where(allowed, ENV_NORM * nt(d_tensor_h, harm), 0.0)
+        yield
         d_weights = d_scalars * tensor + nn(d_around.astype(bf16), harm)
+        yield
         d_latent = d_refined + d_both[0:WIDTH] + nn(w_env[...], d_weights.astype(bf16))
         d_env += jnp.sum(d_latent * act, axis=0, keepdims=True)
         d_pre = (env * d_latent * act_d).astype(bf16)
+        yield
         d_bess = nn(w_basis[...], d_pre)
         both = jnp.concatenate([around.T, d_around.T], axis=1).astype(bf16)
         d_harm = nn(both, jnp.concatenate([d_tensor_h, weights_h], axis=0))
@@ -520,12 +494,18 @@
         moved = jnp.where(place == 2, d_rel[2], moved)
         high = moved.astype(bf16).astype(f32)
         moved_h = jnp.concatenate([high, moved - high], axis=0).astype(bf16)
+        yield
         spread = nt(jnp.concatenate([d_pre, moved_h], axis=0), hot)
         acc[...] += spread[:, 0:HEAD]
         acc_tail[b] = spread[:, HEAD:]
+
+    def several(i, carry):
+        running = [block(abreast * i + k, onehot.at[k]) for k in range(abreast)]
+        while running:
+            running = [r for r in running if next(r, 0) is None]
         return carry
 
-    lax.fori_loop(0, ATOMS // GROUP, block, 0)
+    lax.fori_loop(0, ATOMS // GROUP // abreast, several, 0)
 
 
 def edge_kernel(
@@ -540,7 +520,7 @@
     kind_scale,
     kind_shift,
     w_basis,
-    w_env,
+    env_t,
     w_latent,
     w_out,
     w_final,
@@ -557,7 +537,7 @@
     coords,
     head_proj,
     tail_proj,
-    env_t,
+    env_back,
     latent_t,
     out_t,
     final_col,
@@ -618,7 +598,7 @@
         if end > 128:
             filled[k + 1] = jnp.where(lane < end - 128, value, filled[k + 1])
 
-    env_t[...] = w_env[...].astype(f32).T.astype(bf16)
+    env_back[...] = env_t[...].astype(f32).T.astype(bf16)
     latent_t[...] = w_latent[...].astype(f32).T.astype(bf16)
     out_t[...] = w_out[...].astype(f32).T.astype(bf16)
     final_col[...] = jnp.broadcast_to(column(w_final[...], OUT_WIDTH), (OUT_WIDTH, 128))
@@ -681,7 +661,7 @@
         onehot,
         head_proj,
         tail_proj,
-        w_env,
+        env_back,
         w_latent,
         w_out,
         w_basis,
@@ -778,13 +758,13 @@
             pltpu.VMEM((8, LIST), f32),
             pltpu.VMEM((WIDTH, HEAD), bf16),
             pltpu.VMEM((8, WIDTH, 128), bf16),
-            pltpu.VMEM((3 * CHANNELS, WIDTH), bf16),
+            pltpu.VMEM((WIDTH, 3 * CHANNELS), bf16),
             pltpu.VMEM((WIDTH, WIDTH + 3 * CHANNELS), bf16),
             pltpu.VMEM((OUT_WIDTH, WIDTH), bf16),
             pltpu.VMEM((OUT_WIDTH, 128), f32),
             pltpu.VMEM((6, ATOMS, SLOTS), f32),
             pltpu.VMEM((8, R_COUNT * GROUP, 128), f32),
-            pltpu.VMEM((LIST, GROUP * SLOTS), bf16),
+            pltpu.VMEM((ABREAST, LIST, GROUP * SLOTS), bf16),
             pltpu.VMEM((WIDTH + 16, HEAD), f32),
             pltpu.VMEM((8, WIDTH + 16, 128), f32),
             pltpu.VMEM((ATOMS, 128), f32),
@@ -805,7 +785,8 @@
     proj_grad = own_proj_grad[...]
     pos_grad = jnp.zeros((32, ATOMS), f32)
     atom = rows_of((ATOMS, 128))
-    for i, cell in enumerate(FACE_CELLS):
+    for i, d in enumerate(DIRECTIONS[0:8] + FACES[0:2]):
+        cell = FACE_CELLS[first_face(d)]
         chosen = jnp.where(padded[cell : cell + 1, :] == atom, 1.0, 0.0).astype(bf16)
         proj_grad = proj_grad + nn(chosen[:, 0:GHOST], face_rows[i])
         parts = jnp.concatenate(list(pieces(face_small[i])) + [jnp.zeros((8, 128), f32)], axis=0)
@@ -852,10 +833,9 @@
         w_out,
         w_final,
     ):
-        face_rows, face_small, proj, center = pack(
-            atom_features, positions, send_list, w_center, w_neighbor
+        received, received_small, proj, center = send_out(
+            atom_features, positions, send_list, w_center, w_neighbor, sizes
         )
-        received, received_small = exchange_out(face_rows, face_small, sizes)
         energy, back, back_small, own_proj_grad, center_grad, own_pos_grad = edges(
             received,
             received_small,
@@ -868,14 +848,14 @@
             species_scale,
             species_shift,
             w_basis,
-            w_env,
+            w_env.T,
             w_latent,
             w_out,
             w_final.reshape(1, OUT_WIDTH),
         )
-        face_rows, face_small = exchange_back(back, back_small, sizes)
+        owner_rows, owner_small = send_back(back, back_small, sizes)
         forces, feature_grad = unpack(
-            face_rows, face_small, own_proj_grad, center_grad, own_pos_grad, send_list, w_center, w_neighbor
+            owner_rows, owner_small, own_proj_grad, center_grad, own_pos_grad, send_list, w_center, w_neighbor
         )
         return energy.reshape(ATOMS), forces, feature_grad
 

time: 80.7 us -> 70.6 us (0.87)
  Pallas kernels: 78 us -> 69.8 us
  local copies, waits for them, and re-layouts: 1.66 us -> 0 us
    pallas_call x1, Pallas kernels: 34.6 us -> 28.5 us  [edges(): pl.pallas_call(edge_kernel, out_shape=(jax.ShapeDtypeStruct((1, ATOMS), f...]
    pallas_call x3 -> x2, Pallas kernels: 41.3 us -> 39 us  [the longest x1 20.5 us: send_out(): pl.pallas_call(functools.partial(out_kernel, sizes), out_shape=(jax.Shape...]
    unnamed x1 -> x0, local copies, waits for them, and re-layouts: 1.66 us -> none
where the time goes in v3:
time: 70.6 us; the launch traced here: 70.4 us
  Pallas kernels  69.8 us (99%)
    pallas_call x1, Pallas kernels, edges(): pl.pallas_call(edge_kernel, out_shape=(jax.ShapeDtypeStruct((1, ATOMS), f...  28.5 us
    pallas_call x1, Pallas kernels, send_out(): pl.pallas_call(functools.partial(out_kernel, sizes), out_shape=(jax.Shape...  20.5 us
    pallas_call x1, Pallas kernels, send_back(): pl.pallas_call(functools.partial(back_kernel, sizes), out_shape=(jax.Shap...  18.5 us
    pallas_call x1, Pallas kernels, unpack(): pl.pallas_call(unpack_kernel, out_shape=(jax.ShapeDtypeStruct((3, ATOMS),...  2.25 us

profile of v3, /device:TPU:2, one launch (start us, length us, event | category | flops | bytes accessed | tf_op | source)
XLA Modules:
  0.0 70.4 jit_solution(3757686867518055869)
XLA Ops:
  0.6 20.5 %send_out.1 = (bf16[26,48,256]{2,1,0:T(8,128)(2,1)}, f32[26,8,128]{2,1,0:T(8,128)}, bf16[64,256]{1,0:T(8,128)(2,1)}, bf16[64,256]{1,0:T(8,128)(2,1)}) custom-call(f32[64,256]{1,0:T(8,128)} %features.1, f32[3,64]{1,0:T(4,128)} %positions.3, s32[27,48]{1,0:T(8,128)} %lists.3, bf16[256,256]{1,0:T(8,128)(2,1)} %w_center.3, bf16[256,256]{1,0:T(8,128)(2,1)} %w_neighbor.3), custom_call_target="tpu_custom_call" | custom-call | tf_op jit(solution)/shard_map/send_out/pallas_call | solution.py:216
  21.1 28.5 %edges.1 = (f32[1,64]{1,0:T(1,128)}, bf16[26,48,256]{2,1,0:T(8,128)(2,1)}, f32[26,8,128]{2,1,0:T(8,128)}, f32[64,256]{1,0:T(8,128)}, f32[64,256]{1,0:T(8,128)}, /*index=5*/f32[8,128]{1,0:T(8,128)}) custom-call(bf16[26,48,256]{2,1,0:T(8,128)(2,1)} %get-tuple-element.17.received, f32[26,8,128]{2,1,0:T(8,128)} %get-tuple-element.18.received_small, ...), custom_call_target="tpu_custom_call" | custom-call | tf_op jit(solution)/shard_map/edges/pallas_call | solution.py:741
  49.6 18.5 %send_back.1 = (bf16[10,48,256]{2,1,0:T(8,128)(2,1)}, f32[10,8,128]{2,1,0:T(8,128)}) custom-call(bf16[26,48,256]{2,1,0:T(8,128)(2,1)} %get-tuple-element.22.rows, f32[26,8,128]{2,1,0:T(8,128)} %get-tuple-element.23.small), custom_call_target="tpu_custom_call" | custom-call | tf_op jit(solution)/shard_map/send_back/pallas_call | solution.py:268
  68.2 2.2 %unpack.1 = (f32[3,64]{1,0:T(4,128)}, f32[64,256]{1,0:T(8,128)}) custom-call(bf16[10,48,256]{2,1,0:T(8,128)(2,1)} %get-tuple-element.24.face_rows, f32[10,8,128]{2,1,0:T(8,128)} %get-tuple-element.25.face_small, f32[64,256]{1,0:T(8,128)} %get-tuple-element.26.own_proj_grad, f32[64,256]{1,0:T(8,128)} %get-tuple-element.27.center_grad, ...), custom_call_target="tpu_custom_call" | custom-call | tf_op jit(solution)/shard_map/unpack/pallas_call | solution.py:803

commit v4 on v3

--- a/solution.py
+++ b/solution.py
@@ -26,6 +26,7 @@
 CENTER_AT = 1008
 GROUP = 8
 ABREAST = 4
+SKEW = 1
 
 f32 = jnp.float32
 bf16 = jnp.bfloat16
@@ -238,9 +239,46 @@
 
 
 def back_kernel(
-    sizes, rows, small, owner_rows, owner_small, from_x, from_x_small, total, total_small, send_sem, recv_sem
+    sizes, grad_t, coord_grad, lists, faces, owner_rows, owner_small, grads, rows, small, from_x, from_x_small,
+    total, total_small, send_sem, recv_sem
 ):
     place, barrier = greet(sizes)
+    for k in range(LIST // 128):
+        grads[128 * k : 128 * k + 128, :] = grad_t[:, 128 * k : 128 * k + 128].astype(f32).T
+    face_col = faces[...].T
+    entry, lane = rows_of((GHOST, WIDTH)), lanes_of((8, 128))
+
+    def fill(i):
+        start, count = STARTS[i], SIZES[i]
+        first = min(start, LIST - GHOST)
+        value = grads[first : first + GHOST, :]
+        if first < start:
+            value = jnp.concatenate(
+                [value[start - first : start - first + count], jnp.zeros((GHOST - count, WIDTH), f32)], axis=0
+            )
+        elif count < GHOST:
+            value = jnp.where(entry < count, value, 0.0)
+        value = value.astype(bf16)
+        k, offset = divmod(start, 128)
+        moved = coord_grad[:, 128 * k : 128 * k + 128]
+        if offset:
+            moved = pltpu.roll(moved, 128 - offset, 1)
+        if offset + count > 128:
+            after = pltpu.roll(coord_grad[:, 128 * k + 128 : 128 * k + 256], 128 - offset, 1)
+            moved = jnp.where(lane < 128 - offset, moved, after)
+        moved = jnp.where(lane < count, moved, 0.0)
+        if DIRECTIONS[i] not in FACES:
+            listed = jnp.where(lane[0:1] < count, lists[i : i + 1, :], -1.0)
+            chosen = jnp.where(face_col[:, i : i + 1] == listed, 1.0, 0.0).astype(bf16)
+            value = nn(chosen[0:GHOST, 0:GHOST], value).astype(bf16)
+            parts = jnp.concatenate(list(pieces(moved)) + [jnp.zeros((8, 128), f32)], axis=0)
+            parts = nt(parts.astype(bf16), chosen)
+            moved = parts[0:8] + parts[8:16] + parts[16:24]
+        rows[i] = value
+        small[i] = moved
+
+    for i in range(8, 26):
+        fill(i)
     pl.semaphore_wait(barrier, len(PARTNERS))
     send = sender(place, send_sem, recv_sem)
     given, sums, owners = (rows, small), (total, total_small), (owner_rows, owner_small)
@@ -249,6 +287,8 @@
     x_rest = [send(at(given, X_AT[k] + 3, 6), at(in_x[k], 2, 6), d) for k, d in steps]
     x_pair = [send(at(given, X_AT[k] + 1, 2), at(in_x[k], 0, 2), d) for k, d in steps]
     x_own = [send(at(given, X_AT[k], 1), at(owners, 8 + k, 1), d) for k, d in steps]
+    for i in range(8):
+        fill(i)
     direct = []
     for group, cells in ((x_rest, range(2, 8)), (x_pair, range(2))):
         arrived(*group)
@@ -263,7 +303,7 @@
     sent(*x_rest, *x_pair, *x_own, *direct)
 
 
-def send_back(rows, small, sizes):
+def send_back(grad_t, coord_grad, lists, faces, sizes):
     vmem = pl.BlockSpec(memory_space=pltpu.VMEM)
     return pl.pallas_call(
         functools.partial(back_kernel, sizes),
@@ -271,9 +311,12 @@
             jax.ShapeDtypeStruct((10, GHOST, WIDTH), bf16),
             jax.ShapeDtypeStruct((10, 8, 128), f32),
         ),
-        in_specs=[vmem] * 2,
+        in_specs=[vmem] * 4,
         out_specs=(vmem,) * 2,
         scratch_shapes=[
+            pltpu.VMEM((LIST, WIDTH), f32),
+            pltpu.VMEM((26, GHOST, WIDTH), bf16),
+            pltpu.VMEM((26, 8, 128), f32),
             pltpu.VMEM((2, 8, GHOST, WIDTH), bf16),
             pltpu.VMEM((2, 8, 8, 128), f32),
             pltpu.VMEM((8, GHOST, WIDTH), bf16),
@@ -283,7 +326,7 @@
         ],
         compiler_params=pltpu.CompilerParams(collective_id=1, has_side_effects=True),
         name="send_back",
-    )(rows, small)
+    )(grad_t, coord_grad, lists, faces)
 
 
 R_INDEX, R_ENV, R_SCALED, R_SCALE, R_SLOPE, R_U, R_INV, R_Y, R_BESS, R_BESS_D = 0, 1, 2, 3, 4, 5, 8, 9, 17, 25
@@ -500,9 +543,13 @@
         acc_tail[b] = spread[:, HEAD:]
 
     def several(i, carry):
-        running = [block(abreast * i + k, onehot.at[k]) for k in range(abreast)]
+        running = [(k, block(abreast * i + k, onehot.at[k])) for k in range(abreast)]
+        tick = 0
         while running:
-            running = [r for r in running if next(r, 0) is None]
+            running = [
+                r for r in running if tick < SKEW * r[0] or next(r[1], 0) is None
+            ]
+            tick += 1
         return carry
 
     lax.fori_loop(0, ATOMS // GROUP // abreast, several, 0)
@@ -525,15 +572,14 @@
     w_out,
     w_final,
     energy_out,
-    back,
-    back_small,
+    grad_t,
+    coord_grad,
+    lists,
+    faces,
     own_proj_grad,
     center_grad,
     own_pos_grad,
     rows,
-    tail_rows,
-    lists,
-    faces,
     coords,
     head_proj,
     tail_proj,
@@ -560,7 +606,6 @@
         r = LIST_ROW + FACE_LIST // 2
         faces[i : i + 1, :] = jnp.where(lane[0:1] < GHOST, received_small[i, r : r + 1, :], -2.0)
     entry_col = lists[...].T
-    face_col = faces[...].T
     chosen = {
         i: jnp.where(entry_col[:, i : i + 1] == faces[i : i + 1, :], 1.0, 0.0).astype(bf16) for i in corner
     }
@@ -687,52 +732,19 @@
     tail = acc_tail[0]
     for b in range(1, ATOMS // GROUP):
         tail = tail + acc_tail[b]
-    for k in range(HEAD // 128):
-        rows[128 * k : 128 * k + 128, :] = acc[0:WIDTH, 128 * k : 128 * k + 128].T
-    rows[HEAD:LIST, :] = tail[0:WIDTH].T
-    place = CENTER_AT - HEAD
-    pulled = jnp.zeros((8, 128), f32)
+    grad_t[:, 0:HEAD] = acc[0:WIDTH, :].astype(bf16)
+    grad_t[:, HEAD:LIST] = tail[0:WIDTH].astype(bf16)
+    high, rest = slice(WIDTH, WIDTH + 8), slice(WIDTH + 8, WIDTH + 16)
+    coord_grad[:, 0:HEAD] = acc[high, :] + acc[rest, :]
+    coord_grad[:, HEAD:LIST] = tail[high] + tail[rest]
+    wide = lanes_of((WIDTH + 16, 128))
+    pulled = jnp.zeros((WIDTH + 16, 128), f32)
     for b in range(ATOMS // GROUP):
-        tail_rows[...] = acc_tail[b][0:WIDTH].T
-        center_grad[GROUP * b : GROUP * b + GROUP, :] = tail_rows[place : place + GROUP, :]
-        value = acc_tail[b][WIDTH : WIDTH + 8] + acc_tail[b][WIDTH + 8 : WIDTH + 16]
-        value = pltpu.roll(value, (GROUP * b - place) % 128, 1)
-        pulled = jnp.where((lane >= GROUP * b) & (lane < GROUP * b + GROUP), value, pulled)
-    coord_grad = [
-        acc[WIDTH : WIDTH + 8, 128 * k : 128 * k + 128] + acc[WIDTH + 8 : WIDTH + 16, 128 * k : 128 * k + 128]
-        for k in range(HEAD // 128)
-    ]
-    coord_grad.append(tail[WIDTH : WIDTH + 8] + tail[WIDTH + 8 : WIDTH + 16])
-    own_proj_grad[...] = rows[0:ATOMS, :]
-    own_pos_grad[...] = jnp.where(lane < ATOMS, coord_grad[0] - pulled, 0.0)
-    entry = rows_of((GHOST, WIDTH))
-    for i in range(26):
-        value = rows[STARTS[i] : STARTS[i] + GHOST, :] if STARTS[i] + GHOST <= LIST else None
-        if value is None:
-            tail_rows[0:GHOST, :] = jnp.zeros((GHOST, WIDTH), f32)
-            tail_rows[0 : SIZES[i], :] = rows[STARTS[i] : STARTS[i] + SIZES[i], :]
-            value = tail_rows[0:GHOST, :]
-        elif SIZES[i] < GHOST:
-            value = jnp.where(entry < SIZES[i], value, 0.0)
-        value = value.astype(bf16)
-        if i in chosen:
-            back_chosen = jnp.where(
-                face_col[:, i : i + 1] == jnp.where(lane[0:1] < SIZES[i], lists[i : i + 1, :], -1.0), 1.0, 0.0
-            ).astype(bf16)
-            value = nn(back_chosen[0:GHOST, 0:GHOST], value).astype(bf16)
-        back[i] = value
-        k, at = divmod(STARTS[i], 128)
-        moved = coord_grad[k]
-        if at:
-            moved = pltpu.roll(moved, 128 - at, 1)
-        if at + SIZES[i] > 128:
-            moved = jnp.where(lane < 128 - at, moved, pltpu.roll(coord_grad[k + 1], 128 - at, 1))
-        moved = jnp.where(lane < SIZES[i], moved, 0.0)
-        if i in chosen:
-            parts = jnp.concatenate(list(pieces(moved)) + [jnp.zeros((8, 128), f32)], axis=0)
-            parts = nt(parts.astype(bf16), back_chosen)
-            moved = parts[0:8] + parts[8:16] + parts[16:24]
-        back_small[i] = moved
+        value = pltpu.roll(acc_tail[b], (GROUP * b - (CENTER_AT - HEAD)) % 128, 1)
+        pulled = jnp.where((wide >= GROUP * b) & (wide < GROUP * b + GROUP), value, pulled)
+    center_grad[...] = pulled[0:WIDTH].T[0:ATOMS]
+    own_proj_grad[...] = acc[0:WIDTH, 0:128].T[0:ATOMS]
+    own_pos_grad[...] = jnp.where(lane < ATOMS, coord_grad[:, 0:128] - pulled[high] - pulled[rest], 0.0)
 
 
 def edges(received, received_small, proj, center, positions, species, neighbor, live, scale, shift, *weights):
@@ -742,19 +754,18 @@
         edge_kernel,
         out_shape=(
             jax.ShapeDtypeStruct((1, ATOMS), f32),
-            jax.ShapeDtypeStruct((26, GHOST, WIDTH), bf16),
-            jax.ShapeDtypeStruct((26, 8, 128), f32),
+            jax.ShapeDtypeStruct((WIDTH, LIST), bf16),
+            jax.ShapeDtypeStruct((8, LIST), f32),
+            jax.ShapeDtypeStruct((128, 128), f32),
+            jax.ShapeDtypeStruct((128, 128), f32),
             jax.ShapeDtypeStruct((ATOMS, WIDTH), f32),
             jax.ShapeDtypeStruct((ATOMS, WIDTH), f32),
             jax.ShapeDtypeStruct((8, 128), f32),
         ),
         in_specs=[vmem] * 8 + [smem] * 2 + [vmem] * 5,
-        out_specs=(vmem,) * 6,
+        out_specs=(vmem,) * 8,
         scratch_shapes=[
             pltpu.VMEM((LIST, WIDTH), f32),
-            pltpu.VMEM((128, WIDTH), f32),
-            pltpu.VMEM((128, 128), f32),
-            pltpu.VMEM((128, 128), f32),
             pltpu.VMEM((8, LIST), f32),
             pltpu.VMEM((WIDTH, HEAD), bf16),
             pltpu.VMEM((8, WIDTH, 128), bf16),
@@ -836,7 +847,7 @@
         received, received_small, proj, center = send_out(
             atom_features, positions, send_list, w_center, w_neighbor, sizes
         )
-        energy, back, back_small, own_proj_grad, center_grad, own_pos_grad = edges(
+        energy, grad_t, coord_grad, lists, faces, own_proj_grad, center_grad, own_pos_grad = edges(
             received,
             received_small,
             proj,
@@ -853,7 +864,7 @@
             w_out,
             w_final.reshape(1, OUT_WIDTH),
         )
-        owner_rows, owner_small = send_back(back, back_small, sizes)
+        owner_rows, owner_small = send_back(grad_t, coord_grad, lists, faces, sizes)
         forces, feature_grad = unpack(
             owner_rows, owner_small, own_proj_grad, center_grad, own_pos_grad, send_list, w_center, w_neighbor
         )

time: 70.6 us -> 68.7 us (0.973)
  Pallas kernels: 69.8 us -> 67.9 us
    pallas_call x1, Pallas kernels: 28.5 us -> 26.6 us  [edges(): pl.pallas_call(edge_kernel, out_shape=(jax.ShapeDtypeStruct((1, ATOMS), f...]
where the time goes in v4:
time: 68.7 us; the launch traced here: 68.6 us
  Pallas kernels  67.9 us (99%)
    pallas_call x1, Pallas kernels, edges(): pl.pallas_call(edge_kernel, out_shape=(jax.ShapeDtypeStruct((1, ATOMS), f...  26.6 us
    pallas_call x1, Pallas kernels, send_out(): pl.pallas_call(functools.partial(out_kernel, sizes), out_shape=(jax.Shape...  20.5 us
    pallas_call x1, Pallas kernels, send_back(): pl.pallas_call(functools.partial(back_kernel, sizes), out_shape=(jax.Shap...  18.5 us
    pallas_call x1, Pallas kernels, unpack(): pl.pallas_call(unpack_kernel, out_shape=(jax.ShapeDtypeStruct((3, ATOMS),...  2.25 us

profile of v4, /device:TPU:2, one launch (start us, length us, event | category | flops | bytes accessed | tf_op | source)
XLA Modules:
  0.0 68.6 jit_solution(6704773642332378621)
XLA Ops:
  0.6 20.5 %send_out.1 = (bf16[26,48,256]{2,1,0:T(8,128)(2,1)}, f32[26,8,128]{2,1,0:T(8,128)}, bf16[64,256]{1,0:T(8,128)(2,1)}, bf16[64,256]{1,0:T(8,128)(2,1)}) custom-call(f32[64,256]{1,0:T(8,128)} %features.1, f32[3,64]{1,0:T(4,128)} %positions.3, s32[27,48]{1,0:T(8,128)} %lists.3, bf16[256,256]{1,0:T(8,128)(2,1)} %w_center.3, bf16[256,256]{1,0:T(8,128)(2,1)} %w_neighbor.3), custom_call_target="tpu_custom_call" | custom-call | tf_op jit(solution)/shard_map/send_out/pallas_call | solution.py:217
  21.2 26.6 %edges.1 = (f32[1,64]{1,0:T(1,128)}, bf16[256,1024]{1,0:T(8,128)(2,1)}, f32[8,1024]{1,0:T(8,128)}, f32[128,128]{1,0:T(8,128)}, f32[128,128]{1,0:T(8,128)}, /*ind...) custom-call(bf16[26,48,256]{2,1,0:T(8,128)(2,1)} %get-tuple-element.19.received, ...), custom_call_target="tpu_custom_call" | custom-call | tf_op jit(solution)/shard_map/edges/pallas_call | solution.py:753
  47.8 18.5 %send_back.1 = (bf16[10,48,256]{2,1,0:T(8,128)(2,1)}, f32[10,8,128]{2,1,0:T(8,128)}) custom-call(bf16[256,1024]{1,0:T(8,128)(2,1)} %get-tuple-element.24.grad_t, f32[8,1024]{1,0:T(8,128)} %get-tuple-element.25.coord_grad, f32[128,128]{1,0:T(8,128)} %get-tuple-element.26.lists, f32[128,128]{1,0:T(8,128)} %get-tuple-element.27.faces), custom_call_target="tpu_custom_call" | custom-call | tf_op jit(solution)/shard_map/send_back/pallas_call | solution.py:308
  66.3 2.2 %unpack.1 = (f32[3,64]{1,0:T(4,128)}, f32[64,256]{1,0:T(8,128)}) custom-call(bf16[10,48,256]{2,1,0:T(8,128)(2,1)} %get-tuple-element.28.face_rows, f32[10,8,128]{2,1,0:T(8,128)} %get-tuple-element.29.face_small, f32[64,256]{1,0:T(8,128)} %get-tuple-element.30.own_proj_grad, f32[64,256]{1,0:T(8,128)} %get-tuple-element.31.center_grad, ...), custom_call_target="tpu_custom_call" | custom-call | tf_op jit(solution)/shard_map/unpack/pallas_call | solution.py:814

commit v5 on v4

--- a/solution.py
+++ b/solution.py
@@ -25,6 +25,7 @@
 BASIS_AT = 1000
 CENTER_AT = 1008
 GROUP = 8
+ROWS = 16
 ABREAST = 4
 SKEW = 1
 
@@ -203,11 +204,9 @@
     steps = ((0, FACES[0]), (1, FACES[1]))
     x_own = [send(at(own, X_FACE + k, 1), at(cells, X_AT[k], 1), d) for k, d in steps]
     onward = []
-    for start, count in ((0, 2), (2, 3), (5, 3)):
-        arrived(*[direct[i] for i in range(start, start + count)])
-        onward += [
-            send(at(cells, start, count), at(cells, X_AT[k] + 1 + start, count), d) for k, d in steps
-        ]
+    for i in (0, 1, 2, 5, 3, 4, 6, 7):
+        arrived(direct[i])
+        onward += [send(at(cells, i, 1), at(cells, X_AT[k] + 1 + i, 1), d) for k, d in steps]
     arrived(*x_own, *onward)
     sent(*direct.values(), *x_own, *onward)
 
@@ -230,8 +229,8 @@
             pltpu.VMEM((128, WIDTH), bf16),
             pltpu.VMEM((6, GHOST, WIDTH), bf16),
             pltpu.VMEM((6, 8, 128), f32),
-            pltpu.SemaphoreType.DMA((32,)),
-            pltpu.SemaphoreType.DMA((32,)),
+            pltpu.SemaphoreType.DMA((52,)),
+            pltpu.SemaphoreType.DMA((52,)),
         ],
         compiler_params=pltpu.CompilerParams(collective_id=0, has_side_effects=True),
         name="send_out",
@@ -283,24 +282,27 @@
     send = sender(place, send_sem, recv_sem)
     given, sums, owners = (rows, small), (total, total_small), (owner_rows, owner_small)
     steps = ((0, FACES[1]), (1, FACES[0]))
-    in_x = [(from_x.at[k], from_x_small.at[k]) for k in (0, 1)]
-    x_rest = [send(at(given, X_AT[k] + 3, 6), at(in_x[k], 2, 6), d) for k, d in steps]
-    x_pair = [send(at(given, X_AT[k] + 1, 2), at(in_x[k], 0, 2), d) for k, d in steps]
+    order = (3, 4, 6, 7, 2, 5, 0, 1)
+    x_small = [send([small.at[pl.ds(X_AT[k] + 1, 8)]], [from_x_small.at[k]], d) for k, d in steps]
+    x_cells = {
+        i: [send([rows.at[X_AT[k] + 1 + i]], [from_x.at[k, i]], d) for k, d in steps] for i in order
+    }
     x_own = [send(at(given, X_AT[k], 1), at(owners, 8 + k, 1), d) for k, d in steps]
     for i in range(8):
         fill(i)
+    arrived(*x_small)
+    for i in range(8):
+        total_small[i] = small[i] + from_x_small[0, i] + from_x_small[1, i]
     direct = []
-    for group, cells in ((x_rest, range(2, 8)), (x_pair, range(2))):
-        arrived(*group)
-        for i in cells:
-            total[i] = (
-                rows[i].astype(f32) + from_x[0, i].astype(f32) + from_x[1, i].astype(f32)
-            ).astype(bf16)
-            total_small[i] = small[i] + from_x_small[0, i] + from_x_small[1, i]
-            d = tuple(-t for t in DIRECTIONS[i])
-            direct.append(send(at(sums, i, 1), at(owners, i, 1), d))
+    for i in order:
+        arrived(*x_cells[i])
+        total[i] = (
+            rows[i].astype(f32) + from_x[0, i].astype(f32) + from_x[1, i].astype(f32)
+        ).astype(bf16)
+        d = tuple(-t for t in DIRECTIONS[i])
+        direct.append(send(at(sums, i, 1), at(owners, i, 1), d))
     arrived(*x_own, *direct)
-    sent(*x_rest, *x_pair, *x_own, *direct)
+    sent(*x_small, *[c for i in order for c in x_cells[i]], *x_own, *direct)
 
 
 def send_back(grad_t, coord_grad, lists, faces, sizes):
@@ -321,8 +323,8 @@
             pltpu.VMEM((2, 8, 8, 128), f32),
             pltpu.VMEM((8, GHOST, WIDTH), bf16),
             pltpu.VMEM((8, 8, 128), f32),
-            pltpu.SemaphoreType.DMA((28,)),
-            pltpu.SemaphoreType.DMA((28,)),
+            pltpu.SemaphoreType.DMA((38,)),
+            pltpu.SemaphoreType.DMA((38,)),
         ],
         compiler_params=pltpu.CompilerParams(collective_id=1, has_side_effects=True),
         name="send_back",
@@ -371,6 +373,11 @@
     return [index, env, env * scale, scale, slope, ux, uy, uz, inverse] + ys + bess + bess_d
 
 
+def by_rows(count, step):
+    parts = [step(slice(r, r + ROWS)) for r in range(0, count, ROWS)]
+    return tuple(jnp.concatenate(p, axis=0) for p in zip(*parts))
+
+
 def edge_blocks(
     per_atom,
     slots,
@@ -458,14 +465,16 @@
 
         yield
         pre = nn(jnp.concatenate([head_proj[...], tail_proj[b]], axis=1), hot)
-        sig = sigmoid(pre)
-        act = pre * sig
-        act_d = sig + act * (1.0 - sig)
-        latent = env * act
-        latent_h = latent.astype(bf16)
+
+        def first(r):
+            sig = sigmoid(pre[r])
+            act = pre[r] * sig
+            return act, sig + act * (1.0 - sig), (env * act).astype(bf16)
+
+        act, act_d, latent_h = by_rows(WIDTH, first)
         yield
         weights = nn(env_t[...], latent_h)
-        weights_h = weights.astype(bf16)
+        (weights_h,) = by_rows(3 * CHANNELS, lambda r: (weights[r].astype(bf16),))
         ys = eight(R_Y)
         harm = jnp.concatenate(
             [maskf]
@@ -478,42 +487,63 @@
         around_h = around.astype(bf16)
         yield
         tensor = nn(around_h, harm)
-        scalars_h = (weights * tensor).astype(bf16)
+        (scalars_h,) = by_rows(3 * CHANNELS, lambda r: ((weights[r] * tensor[r]).astype(bf16),))
         yield
         mixed = nn(latent_t[...], jnp.concatenate([latent_h, scalars_h], axis=0))
-        sig = sigmoid(mixed)
-        update = mixed * sig
-        update_d = sig + update * (1.0 - sig)
-        refined_h = (latent + env * update).astype(bf16)
+
+        def second(r):
+            sig = sigmoid(mixed[r])
+            update = mixed[r] * sig
+            return update, sig + update * (1.0 - sig), (env * (act[r] + update)).astype(bf16)
+
+        update, update_d, refined_h = by_rows(WIDTH, second)
         yield
         hidden = nn(out_t[...], refined_h)
-        sig = sigmoid(hidden)
-        hidden_act = hidden * sig
-        final = final_col[:, 0:1]
-        per_edge = jnp.sum(hidden_act * final, axis=0, keepdims=True)
+        scaled = value(R_SCALED)
+        sums = [jnp.zeros((ROWS, width), f32) for _ in range(3)]
+
+        def third(r):
+            sig = sigmoid(hidden[r])
+            hidden_act = hidden[r] * sig
+            final = final_col[r, 0:1]
+            sums[0] = sums[0] + hidden_act * final
+            return (((sig + hidden_act * (1.0 - sig)) * final * scaled).astype(bf16),)
+
+        (d_hidden,) = by_rows(OUT_WIDTH, third)
+        per_edge = jnp.sum(sums[0], axis=0, keepdims=True)
         energy[pl.ds(pl.multiple_of(b * GROUP, GROUP), GROUP), :] = jnp.broadcast_to(
             jnp.sum(maskf * (env * per_edge), axis=1, keepdims=True), (GROUP, 128)
         )
 
-        scaled = value(R_SCALED)
-        d_hidden = ((sig + hidden_act * (1.0 - sig)) * final * scaled).astype(bf16)
         yield
         d_refined = nn(w_out[...], d_hidden)
-        d_env = value(R_SCALE) * per_edge
-        d_env += jnp.sum(d_refined * update, axis=0, keepdims=True)
-        d_mixed = (env * d_refined * update_d).astype(bf16)
+
+        def fourth(r):
+            sums[1] = sums[1] + d_refined[r] * update[r]
+            return ((env * d_refined[r] * update_d[r]).astype(bf16),)
+
+        (d_mixed,) = by_rows(WIDTH, fourth)
         yield
         d_both = nn(w_latent[...], d_mixed)
         d_scalars = d_both[WIDTH:]
-        d_tensor_h = (d_scalars * weights).astype(bf16)
+        (d_tensor_h,) = by_rows(3 * CHANNELS, lambda r: ((d_scalars[r] * weights[r]).astype(bf16),))
         yield
         d_around = jnp.where(allowed, ENV_NORM * nt(d_tensor_h, harm), 0.0)
         yield
-        d_weights = d_scalars * tensor + nn(d_around.astype(bf16), harm)
-        yield
-        d_latent = d_refined + d_both[0:WIDTH] + nn(w_env[...], d_weights.astype(bf16))
-        d_env += jnp.sum(d_latent * act, axis=0, keepdims=True)
-        d_pre = (env * d_latent * act_d).astype(bf16)
+        around_grad = nn(d_around.astype(bf16), harm)
+        (d_weights,) = by_rows(
+            3 * CHANNELS, lambda r: ((d_scalars[r] * tensor[r] + around_grad[r]).astype(bf16),)
+        )
+        yield
+        from_weights = nn(w_env[...], d_weights)
+
+        def fifth(r):
+            d_latent = d_refined[r] + d_both[r] + from_weights[r]
+            sums[2] = sums[2] + d_latent * act[r]
+            return ((env * d_latent * act_d[r]).astype(bf16),)
+
+        (d_pre,) = by_rows(WIDTH, fifth)
+        d_env = value(R_SCALE) * per_edge + jnp.sum(sums[1] + sums[2], axis=0, keepdims=True)
         yield
         d_bess = nn(w_basis[...], d_pre)
         both = jnp.concatenate([around.T, d_around.T], axis=1).astype(bf16)

time: 68.7 us -> 68.2 us (level)
  no operation moved by 1% of the time
where the time goes in v5:
time: 68.2 us; the launch traced here: 68 us
  Pallas kernels  67.3 us (99%)
    pallas_call x1, Pallas kernels, edges(): pl.pallas_call(edge_kernel, out_shape=(jax.ShapeDtypeStruct((1, ATOMS), f...  26.3 us
    pallas_call x1, Pallas kernels, send_out(): pl.pallas_call(functools.partial(out_kernel, sizes), out_shape=(jax.Shape...  20.6 us
    pallas_call x1, Pallas kernels, send_back(): pl.pallas_call(functools.partial(back_kernel, sizes), out_shape=(jax.Shap...  18.2 us
    pallas_call x1, Pallas kernels, unpack(): pl.pallas_call(unpack_kernel, out_shape=(jax.ShapeDtypeStruct((3, ATOMS),...  2.25 us

profile of v5, /device:TPU:2, one launch (start us, length us, event | category | flops | bytes accessed | tf_op | source)
XLA Modules:
  0.0 68.0 jit_solution(14803833524069800804)
XLA Ops:
  0.6 20.6 %send_out.1 = (bf16[26,48,256]{2,1,0:T(8,128)(2,1)}, f32[26,8,128]{2,1,0:T(8,128)}, bf16[64,256]{1,0:T(8,128)(2,1)}, bf16[64,256]{1,0:T(8,128)(2,1)}) custom-call(f32[64,256]{1,0:T(8,128)} %features.1, f32[3,64]{1,0:T(4,128)} %positions.3, s32[27,48]{1,0:T(8,128)} %lists.3, bf16[256,256]{1,0:T(8,128)(2,1)} %w_center.3, bf16[256,256]{1,0:T(8,128)(2,1)} %w_neighbor.3), custom_call_target="tpu_custom_call" | custom-call | tf_op jit(solution)/shard_map/send_out/pallas_call | solution.py:216
  21.2 26.3 %edges.1 = (f32[1,64]{1,0:T(1,128)}, bf16[256,1024]{1,0:T(8,128)(2,1)}, f32[8,1024]{1,0:T(8,128)}, f32[128,128]{1,0:T(8,128)}, f32[128,128]{1,0:T(8,128)}, /*ind...) custom-call(bf16[26,48,256]{2,1,0:T(8,128)(2,1)} %get-tuple-element.19.received, ...), custom_call_target="tpu_custom_call" | custom-call | tf_op jit(solution)/shard_map/edges/pallas_call | solution.py:783
  47.5 18.2 %send_back.1 = (bf16[10,48,256]{2,1,0:T(8,128)(2,1)}, f32[10,8,128]{2,1,0:T(8,128)}) custom-call(bf16[256,1024]{1,0:T(8,128)(2,1)} %get-tuple-element.24.grad_t, f32[8,1024]{1,0:T(8,128)} %get-tuple-element.25.coord_grad, f32[128,128]{1,0:T(8,128)} %get-tuple-element.26.lists, f32[128,128]{1,0:T(8,128)} %get-tuple-element.27.faces), custom_call_target="tpu_custom_call" | custom-call | tf_op jit(solution)/shard_map/send_back/pallas_call | solution.py:310
  65.7 2.2 %unpack.1 = (f32[3,64]{1,0:T(4,128)}, f32[64,256]{1,0:T(8,128)}) custom-call(bf16[10,48,256]{2,1,0:T(8,128)(2,1)} %get-tuple-element.28.face_rows, f32[10,8,128]{2,1,0:T(8,128)} %get-tuple-element.29.face_small, f32[64,256]{1,0:T(8,128)} %get-tuple-element.30.own_proj_grad, f32[64,256]{1,0:T(8,128)} %get-tuple-element.31.center_grad, ...), custom_call_target="tpu_custom_call" | custom-call | tf_op jit(solution)/shard_map/unpack/pallas_call | solution.py:844
